TPU v7x, 256 devices: a whole 4x4x8 slice. The times are simulated.
256 devices in a mesh: panel: 4 (over y), front: 64 (over x, z, core).
Axes of the slice: x: 4, y: 4, z: 8, core: 2. Of those that a mesh axis runs over, the one named last changes fastest.
Arguments:
- leaf_rhs: float32 [4, 64, 2, 32, 1280], P('panel', 'front'), may hold values from -6 to 6
- sep_rhs: float32 [4, 2, 32, 1024], P('panel', None, None, 'front'), may hold values from -6 to 6
- leaf_inverse: bfloat16 [4, 64, 2, 1280, 1280], P('panel', 'front'), may hold values from -0.15625 to 0.15625
- coupling: bfloat16 [4, 64, 2, 1280, 128], P('panel', 'front'), may hold values from -0.15625 to 0.15625
- sep_index: int32 [4, 64, 128], P('panel', 'front'), may hold values from 0 to 1023, as said below
- sep_inverse: bfloat16 [4, 2, 1024, 1024], P('panel', None, None, 'front'), may hold values from -0.1875 to 0.1875
Outputs:
- leaf_solution: float32 [4, 64, 2, 32, 1280], P('panel', 'front')
- sep_solution: float32 [4, 2, 32, 1024], P('panel', None, None, 'front')
Inputs may be any that keep to these rules, and one draw needn't show every extreme that they name: `sep_index`: within one leaf no separator unknown repeats, and every separator unknown of a panel is coupled to exactly 8 leaves.
All inputs are finite; a program needn't handle non-finite values.
Results may differ from a plain program's by a relative error of at most 0.035.
Values may be sent and summed in bfloat16 or wider, within the bound.
A program may use at most 64 MiB of HBM per device.

v0:
```python
import jax
import jax.numpy as jnp
from jax import lax
from jax.sharding import PartitionSpec as P

LAYER = 128


def shifted(value, axis, by):
    length = lax.axis_size(axis)
    pairs = [(i, i + by) for i in range(length) if 0 <= i + by < length]
    return lax.ppermute(value, axis, pairs)


def complex_rows(vector, matrix):
    count = vector.shape[1]
    flat = vector.reshape(2 * count, vector.shape[2])
    real_part = jnp.dot(flat, matrix[0], preferred_element_type=jnp.float32)
    imag_part = jnp.dot(flat, matrix[1], preferred_element_type=jnp.float32)
    return jnp.stack([real_part[:count] - imag_part[count:], imag_part[:count] + real_part[count:]])


def complex_rows_back(vector, matrix):
    count = vector.shape[1]
    flat = vector.reshape(2 * count, vector.shape[2])
    dims = (((1,), (1,)), ((), ()))
    real_part = lax.dot_general(flat, matrix[0], dims, preferred_element_type=jnp.float32)
    imag_part = lax.dot_general(flat, matrix[1], dims, preferred_element_type=jnp.float32)
    return jnp.stack([real_part[:count] - imag_part[count:], imag_part[:count] + real_part[count:]])


def local(leaf_rhs, sep_rhs, leaf_inverse, coupling, sep_index, sep_inverse):
    inverse = leaf_inverse[0, 0]
    linkage = coupling[0, 0]
    index = sep_index[0, 0]
    sep_matrix = sep_inverse[0]
    leaf_local = leaf_rhs[0, 0]
    sep_local = sep_rhs[0]
    fronts = lax.axis_size("front")
    panels = lax.axis_size("panel")
    panel_at = lax.axis_index("panel")
    sep_width = sep_local.shape[2]
    sep_whole = sep_width * fronts
    rhs_count = leaf_local.shape[1]
    cells = leaf_local.shape[2]
    groups = 1
    rows_group = rhs_count // groups

    def solve(leaf_side, sep_side):
        first = complex_rows(leaf_side.astype(jnp.bfloat16), inverse)
        toward = complex_rows(first.astype(jnp.bfloat16), linkage)
        summed = jnp.zeros((2, rows_group, sep_whole), jnp.float32).at[:, :, index].add(toward)
        share = lax.psum_scatter(summed, "front", scatter_dimension=2, tiled=True)
        reduced = lax.all_gather(
            (sep_side - share).astype(jnp.bfloat16), "front", axis=2, tiled=True
        )
        sep_sol = complex_rows(reduced, sep_matrix)
        sep_full = lax.all_gather(sep_sol.astype(jnp.bfloat16), "front", axis=2, tiled=True)
        picked = sep_full[:, :, index]
        back = complex_rows_back(picked, linkage)
        corr = complex_rows(back.astype(jnp.bfloat16), inverse)
        return (first - corr, sep_sol)

    def forward_step(step, carry):
        leaf_store, sep_store, outgoing = carry
        incoming = shifted(outgoing, "panel", 1)
        group = step - panel_at
        active = (group >= 0) & (group < groups)
        leaf_side = leaf_local
        leaf_side = leaf_side.at[:, :, :LAYER].add(incoming)
        leaf_sol, sep_sol = solve(leaf_side, sep_local)
        old_leaf = leaf_store
        old_sep = sep_store
        leaf_store = jnp.where(active, leaf_sol, old_leaf)
        sep_store = jnp.where(active, sep_sol, old_sep)
        return (leaf_store, sep_store, leaf_sol[:, :, cells - LAYER :])

    steps_total = panels + groups - 1
    start_layer = jnp.zeros((2, rows_group, LAYER), jnp.float32)
    forward_leaf, forward_sep, unused = lax.fori_loop(
        0,
        steps_total,
        forward_step,
        (jnp.zeros_like(leaf_local), jnp.zeros_like(sep_local), start_layer),
    )
    is_last = panel_at == panels - 1

    def backward_step(step, carry):
        leaf_store, sep_store, outgoing = carry
        incoming = shifted(outgoing.astype(jnp.bfloat16), "panel", -1).astype(outgoing.dtype)
        group = jnp.where(is_last, step + 1, step - (panels - 2 - panel_at))
        active = (group >= 0) & (group < groups)
        solving = active & jnp.logical_not(is_last)
        leaf_side = (
            jnp.zeros((2, rows_group, cells), jnp.float32).at[:, :, cells - LAYER :].set(incoming)
        )
        sep_side = jnp.zeros((2, rows_group, sep_width), jnp.float32)
        leaf_sol, sep_sol = solve(leaf_side, sep_side)
        leaf_sol = jnp.where(is_last, 0.0, leaf_sol)
        sep_sol = jnp.where(is_last, 0.0, sep_sol)
        leaf_new = forward_leaf + leaf_sol
        sep_new = forward_sep + sep_sol
        old_leaf = leaf_store
        old_sep = sep_store
        leaf_store = jnp.where(solving, leaf_new, old_leaf)
        sep_store = jnp.where(solving, sep_new, old_sep)
        return (leaf_store, sep_store, leaf_new[:, :, :LAYER])

    steps_back = panels - 1 + groups - 1
    first_face = jnp.where(is_last, forward_leaf[:, :rows_group, :LAYER], start_layer)
    final_leaf, final_sep, unused_back = lax.fori_loop(
        0, steps_back, backward_step, (forward_leaf, forward_sep, first_face)
    )
    return (final_leaf[None, None], final_sep[None])


def solution(mesh):
    in_specs = (
        P("panel", "front", None, None, None),
        P("panel", None, None, "front"),
        P("panel", "front", None, None, None),
        P("panel", "front", None, None, None),
        P("panel", "front", None),
        P("panel", None, None, "front"),
    )
    out_specs = (P("panel", "front", None, None, None), P("panel", None, None, "front"))
    return jax.shard_map(local, mesh=mesh, in_specs=in_specs, out_specs=out_specs, check_vma=False)
```

profile of v0, /device:TPU:1, one launch (start us, length us, event | category | flops | bytes accessed | tf_op | source)
XLA Modules:
  0.0 1978.4 jit_solution(4215934631477807635)
XLA Ops:
  9.7 1212.0 %while.42 = (s32[]{:T(128)}, f32[2,32,1280]{2,1,0:T(8,128)S(1)}, f32[2,32,16]{1,2,0:T(8,128)S(1)}, f32[2,32,128]{2,1,0:T(8,128)S(1)}, s32[]{:T(128)}, /*index=5*...) while((s32[]{:T(128)}, f32[2,32,1280]{2,1,0:T(8,128)S(1)}, ...), condition=%wide.region_3.4_spmd.clone, body=%wide.region_0.3_spmd.clone.sunk | while | flops 927949184 | bytes 32242636 | solution.py:80
  9.8 4.2 collective-permute-start.1
  15.0 2.6 fusion.250
  17.6 2.6 fusion.251
  21.2 4.9 scatter_fusion.1
  28.3 187.2 %all-reduce.6.cloned.1.call-done = f32[2,32,1024]{1,0,2:T(2,128)} async-done(((f32[2,32,1024]{1,0,2:T(2,128)}), f32[2,32,1024]{1,0,2:T(2,128)}) %all-reduce.6.cloned.1.call-update) | async-done | bytes 262160 | tf_op jit(solution)/shard_map/while
  216.2 50.9 %all_gather.48 = bf16[2,32,1024]{1,0,2:T(2,128)(2,1)S(1)} all-gather(bf16[2,32,16]{1,0,2:T(2,128)(2,1)S(1)} %fusion.257), channel_id=1, replica_groups=mesh['panel'=4,'front'=64] {'front'}, dimensions={2}, use_global_device_ids=true | all-gather | bytes 133120 | tf_op jit(solution)/shard_map/while/body/eval_jaxpr/all_gather | solution.py:54
  267.9 42.6 %all_gather.49 = bf16[2,32,1024]{1,2,0:T(8,128)(2,1)S(1)} all-gather(bf16[2,32,16]{1,2,0:T(8,128)(2,1)S(1)} %fusion.261), channel_id=1, replica_groups=mesh['panel'=4,'front'=64] {'front'}, dimensions={2}, use_global_device_ids=true | all-gather | bytes 133120 | tf_op jit(solution)/shard_map/while/body/eval_jaxpr/all_gather | solution.py:58
  315.0 2.6 fusion.266
  317.9 3.2 collective-permute-start.1
  322.2 2.6 fusion.250
  324.9 2.6 fusion.251
  328.4 4.9 scatter_fusion.1
  335.6 181.2 %all-reduce.6.cloned.1.call-done = f32[2,32,1024]{1,0,2:T(2,128)} async-done(((f32[2,32,1024]{1,0,2:T(2,128)}), f32[2,32,1024]{1,0,2:T(2,128)}) %all-reduce.6.cloned.1.call-update) | async-done | bytes 262160 | tf_op jit(solution)/shard_map/while
  517.5 50.9 %all_gather.48 = bf16[2,32,1024]{1,0,2:T(2,128)(2,1)S(1)} all-gather(bf16[2,32,16]{1,0,2:T(2,128)(2,1)S(1)} %fusion.257), channel_id=1, replica_groups=mesh['panel'=4,'front'=64] {'front'}, dimensions={2}, use_global_device_ids=true | all-gather | bytes 133120 | tf_op jit(solution)/shard_map/while/body/eval_jaxpr/all_gather | solution.py:54
  569.2 42.6 %all_gather.49 = bf16[2,32,1024]{1,2,0:T(8,128)(2,1)S(1)} all-gather(bf16[2,32,16]{1,2,0:T(8,128)(2,1)S(1)} %fusion.261), channel_id=1, replica_groups=mesh['panel'=4,'front'=64] {'front'}, dimensions={2}, use_global_device_ids=true | all-gather | bytes 133120 | tf_op jit(solution)/shard_map/while/body/eval_jaxpr/all_gather | solution.py:58
  616.3 2.6 fusion.266
  619.2 3.2 collective-permute-start.1
  623.5 2.6 fusion.250
  626.2 2.6 fusion.251
  629.7 4.9 scatter_fusion.1
  636.8 181.2 %all-reduce.6.cloned.1.call-done = f32[2,32,1024]{1,0,2:T(2,128)} async-done(((f32[2,32,1024]{1,0,2:T(2,128)}), f32[2,32,1024]{1,0,2:T(2,128)}) %all-reduce.6.cloned.1.call-update) | async-done | bytes 262160 | tf_op jit(solution)/shard_map/while
  818.8 50.9 %all_gather.48 = bf16[2,32,1024]{1,0,2:T(2,128)(2,1)S(1)} all-gather(bf16[2,32,16]{1,0,2:T(2,128)(2,1)S(1)} %fusion.257), channel_id=1, replica_groups=mesh['panel'=4,'front'=64] {'front'}, dimensions={2}, use_global_device_ids=true | all-gather | bytes 133120 | tf_op jit(solution)/shard_map/while/body/eval_jaxpr/all_gather | solution.py:54
  870.5 42.6 %all_gather.49 = bf16[2,32,1024]{1,2,0:T(8,128)(2,1)S(1)} all-gather(bf16[2,32,16]{1,2,0:T(8,128)(2,1)S(1)} %fusion.261), channel_id=1, replica_groups=mesh['panel'=4,'front'=64] {'front'}, dimensions={2}, use_global_device_ids=true | all-gather | bytes 133120 | tf_op jit(solution)/shard_map/while/body/eval_jaxpr/all_gather | solution.py:58
  920.5 3.2 collective-permute-start.1
  924.8 2.6 fusion.250
  927.5 2.6 fusion.251
  931.0 4.9 scatter_fusion.1
  938.1 181.2 %all-reduce.6.cloned.1.call-done = f32[2,32,1024]{1,0,2:T(2,128)} async-done(((f32[2,32,1024]{1,0,2:T(2,128)}), f32[2,32,1024]{1,0,2:T(2,128)}) %all-reduce.6.cloned.1.call-update) | async-done | bytes 262160 | tf_op jit(solution)/shard_map/while
  1120.1 50.9 %all_gather.48 = bf16[2,32,1024]{1,0,2:T(2,128)(2,1)S(1)} all-gather(bf16[2,32,16]{1,0,2:T(2,128)(2,1)S(1)} %fusion.257), channel_id=1, replica_groups=mesh['panel'=4,'front'=64] {'front'}, dimensions={2}, use_global_device_ids=true | all-gather | bytes 133120 | tf_op jit(solution)/shard_map/while/body/eval_jaxpr/all_gather | solution.py:54
  1171.8 42.6 %all_gather.49 = bf16[2,32,1024]{1,2,0:T(8,128)(2,1)S(1)} all-gather(bf16[2,32,16]{1,2,0:T(8,128)(2,1)S(1)} %fusion.261), channel_id=1, replica_groups=mesh['panel'=4,'front'=64] {'front'}, dimensions={2}, use_global_device_ids=true | all-gather | bytes 133120 | tf_op jit(solution)/shard_map/while/body/eval_jaxpr/all_gather | solution.py:58
  1221.8 749.1 %while.41 = (s32[]{:T(128)}, f32[2,32,1280]{2,1,0:T(8,128)S(1)}, f32[2,32,16]{1,2,0:T(8,128)S(1)}, bf16[2,32,128]{2,1,0:T(8,128)(2,1)S(1)}, s32[]{:T(128)}, /*in...) while((s32[]{:T(128)}, f32[2,32,1280]{2,1,0:T(8,128)S(1)}, ...), condition=%wide.region_7.8_spmd, body=%wide.region_4.0_spmd.sunk | while | flops 928040320 | bytes 29985640 | solution.py:111
  1229.3 2.6 fusion.213
  1232.9 4.9 scatter_fusion
  1238.9 132.4 %reduce-scatter.2.cloned.1.call-done = f32[2,32,16]{1,2,0:T(8,128)} async-done(((f32[2,32,1024]{1,2,0:T(8,128)}), f32[2,32,16]{1,2,0:T(8,128)}) %reduce-scatter.2.cloned.1.call-update) | async-done | bytes 4112 | tf_op jit(solution)/shard_map/while/body/eval_jaxpr/reduce_scatter | solution.py:53
  1372.1 48.5 %all_gather.46 = bf16[2,32,1024]{1,2,0:T(8,128)(2,1)S(1)} all-gather(bf16[2,32,16]{1,2,0:T(8,128)(2,1)S(1)} %subtract_convert_fusion.2), channel_id=1, replica_groups=mesh['panel'=4,'front'=64] {'front'}, dimensions={2}, use_global_device_ids=true | all-gather | bytes 133120 | tf_op jit(solution)/shard_map/while/body/eval_jaxpr/all_gather | solution.py:54
  1421.2 42.4 %all_gather.47 = bf16[2,32,1024]{1,2,0:T(8,128)(2,1)S(1)} all-gather(bf16[2,32,16]{1,2,0:T(8,128)(2,1)S(1)} %fusion.222), channel_id=1, replica_groups=mesh['panel'=4,'front'=64] {'front'}, dimensions={2}, use_global_device_ids=true | all-gather | bytes 133120 | tf_op jit(solution)/shard_map/while/body/eval_jaxpr/all_gather | solution.py:58
  1478.3 2.6 fusion.213
  1481.9 4.9 scatter_fusion
  1487.9 133.0 %reduce-scatter.2.cloned.1.call-done = f32[2,32,16]{1,2,0:T(8,128)} async-done(((f32[2,32,1024]{1,2,0:T(8,128)}), f32[2,32,16]{1,2,0:T(8,128)}) %reduce-scatter.2.cloned.1.call-update) | async-done | bytes 4112 | tf_op jit(solution)/shard_map/while/body/eval_jaxpr/reduce_scatter | solution.py:53
  1621.7 48.8 %all_gather.46 = bf16[2,32,1024]{1,2,0:T(8,128)(2,1)S(1)} all-gather(bf16[2,32,16]{1,2,0:T(8,128)(2,1)S(1)} %subtract_convert_fusion.2), channel_id=1, replica_groups=mesh['panel'=4,'front'=64] {'front'}, dimensions={2}, use_global_device_ids=true | all-gather | bytes 133120 | tf_op jit(solution)/shard_map/while/body/eval_jaxpr/all_gather | solution.py:54
  1671.1 42.4 %all_gather.47 = bf16[2,32,1024]{1,2,0:T(8,128)(2,1)S(1)} all-gather(bf16[2,32,16]{1,2,0:T(8,128)(2,1)S(1)} %fusion.222), channel_id=1, replica_groups=mesh['panel'=4,'front'=64] {'front'}, dimensions={2}, use_global_device_ids=true | all-gather | bytes 133120 | tf_op jit(solution)/shard_map/while/body/eval_jaxpr/all_gather | solution.py:58
  1728.2 2.6 fusion.213
  1731.8 4.9 scatter_fusion
  1737.9 133.4 %reduce-scatter.2.cloned.1.call-done = f32[2,32,16]{1,2,0:T(8,128)} async-done(((f32[2,32,1024]{1,2,0:T(8,128)}), f32[2,32,16]{1,2,0:T(8,128)}) %reduce-scatter.2.cloned.1.call-update) | async-done | bytes 4112 | tf_op jit(solution)/shard_map/while/body/eval_jaxpr/reduce_scatter | solution.py:53
  1871.9 48.5 %all_gather.46 = bf16[2,32,1024]{1,2,0:T(8,128)(2,1)S(1)} all-gather(bf16[2,32,16]{1,2,0:T(8,128)(2,1)S(1)} %subtract_convert_fusion.2), channel_id=1, replica_groups=mesh['panel'=4,'front'=64] {'front'}, dimensions={2}, use_global_device_ids=true | all-gather | bytes 133120 | tf_op jit(solution)/shard_map/while/body/eval_jaxpr/all_gather | solution.py:54
  1921.1 42.4 %all_gather.47 = bf16[2,32,1024]{1,2,0:T(8,128)(2,1)S(1)} all-gather(bf16[2,32,16]{1,2,0:T(8,128)(2,1)S(1)} %fusion.222), channel_id=1, replica_groups=mesh['panel'=4,'front'=64] {'front'}, dimensions={2}, use_global_device_ids=true | all-gather | bytes 133120 | tf_op jit(solution)/shard_map/while/body/eval_jaxpr/all_gather | solution.py:58
  1968.0 2.6 fusion.227
  (302 shorter events, 98.3 us)
Async XLA Ops:
  9.7 10.6 copy-start
  9.7 205.8 %all-reduce.6.cloned.1.call-start = ((), (), s32[]{:S(2)}) async-start(), calls=%async_computation.2 | async-start | bytes 2097152 | tf_op jit(solution)/shard_map/while
  9.8 5.2 collective-permute-start.1
  14.6 12.5 copy-start.7
  15.0 252.6 %copy-start.4 = (bf16[2,1024,16]{1,2,0:T(8,128)(2,1)S(1)}, bf16[2,1024,16]{1,2,0:T(8,128)(2,1)}, u32[]{:S(2)}) copy-start(bf16[2,1024,16]{1,2,0:T(8,128)(2,1)} %get-tuple-element.979) | copy-start | bytes 196612 | tf_op jit(solution)/shard_map/while
  26.1 1.0 copy-start.2
  317.9 9.7 copy-start
  317.9 198.9 %all-reduce.6.cloned.1.call-start = ((), (), s32[]{:S(2)}) async-start(), calls=%async_computation.2 | async-start | bytes 2097152 | tf_op jit(solution)/shard_map/while
  317.9 4.3 collective-permute-start.1
  321.9 12.5 copy-start.7
  322.2 246.6 %copy-start.4 = (bf16[2,1024,16]{1,2,0:T(8,128)(2,1)S(1)}, bf16[2,1024,16]{1,2,0:T(8,128)(2,1)}, u32[]{:S(2)}) copy-start(bf16[2,1024,16]{1,2,0:T(8,128)(2,1)} %get-tuple-element.979) | copy-start | bytes 196612 | tf_op jit(solution)/shard_map/while
  333.3 1.0 copy-start.2
  619.2 9.7 copy-start
  619.2 198.9 %all-reduce.6.cloned.1.call-start = ((), (), s32[]{:S(2)}) async-start(), calls=%async_computation.2 | async-start | bytes 2097152 | tf_op jit(solution)/shard_map/while
  619.2 4.3 collective-permute-start.1
  623.2 12.5 copy-start.7
  623.5 246.6 %copy-start.4 = (bf16[2,1024,16]{1,2,0:T(8,128)(2,1)S(1)}, bf16[2,1024,16]{1,2,0:T(8,128)(2,1)}, u32[]{:S(2)}) copy-start(bf16[2,1024,16]{1,2,0:T(8,128)(2,1)} %get-tuple-element.979) | copy-start | bytes 196612 | tf_op jit(solution)/shard_map/while
  634.6 1.0 copy-start.2
  920.5 9.7 copy-start
  920.5 198.9 %all-reduce.6.cloned.1.call-start = ((), (), s32[]{:S(2)}) async-start(), calls=%async_computation.2 | async-start | bytes 2097152 | tf_op jit(solution)/shard_map/while
  920.5 4.3 collective-permute-start.1
  924.4 12.5 copy-start.7
  924.8 246.6 %copy-start.4 = (bf16[2,1024,16]{1,2,0:T(8,128)(2,1)S(1)}, bf16[2,1024,16]{1,2,0:T(8,128)(2,1)}, u32[]{:S(2)}) copy-start(bf16[2,1024,16]{1,2,0:T(8,128)(2,1)} %get-tuple-element.979) | copy-start | bytes 196612 | tf_op jit(solution)/shard_map/while
  935.9 1.0 copy-start.2
  1222.0 10.1 copy-start.1
  1222.0 149.3 %reduce-scatter.2.cloned.1.call-start = ((), (), s32[]{:S(2)}) async-start(), calls=%async_computation.1 | async-start | bytes 1064960 | tf_op jit(solution)/shard_map/while/body/eval_jaxpr/reduce_scatter | solution.py:53
  1222.1 4.6 collective-permute-start
  1229.3 191.5 %copy-start.5 = (bf16[2,1024,16]{1,2,0:T(8,128)(2,1)S(1)}, bf16[2,1024,16]{1,2,0:T(8,128)(2,1)}, u32[]{:S(2)}) copy-start(bf16[2,1024,16]{1,2,0:T(8,128)(2,1)} %get-tuple-element.1030) | copy-start | bytes 196612 | tf_op jit(solution)/shard_map/while
  1471.0 10.1 copy-start.1
  1471.0 150.0 %reduce-scatter.2.cloned.1.call-start = ((), (), s32[]{:S(2)}) async-start(), calls=%async_computation.1 | async-start | bytes 1064960 | tf_op jit(solution)/shard_map/while/body/eval_jaxpr/reduce_scatter | solution.py:53
  1471.1 4.6 collective-permute-start
  1478.3 192.4 %copy-start.5 = (bf16[2,1024,16]{1,2,0:T(8,128)(2,1)S(1)}, bf16[2,1024,16]{1,2,0:T(8,128)(2,1)}, u32[]{:S(2)}) copy-start(bf16[2,1024,16]{1,2,0:T(8,128)(2,1)} %get-tuple-element.1030) | copy-start | bytes 196612 | tf_op jit(solution)/shard_map/while
  1720.9 10.1 copy-start.1
  1720.9 150.3 %reduce-scatter.2.cloned.1.call-start = ((), (), s32[]{:S(2)}) async-start(), calls=%async_computation.1 | async-start | bytes 1064960 | tf_op jit(solution)/shard_map/while/body/eval_jaxpr/reduce_scatter | solution.py:53
  1721.0 4.6 collective-permute-start
  1728.2 192.4 %copy-start.5 = (bf16[2,1024,16]{1,2,0:T(8,128)(2,1)S(1)}, bf16[2,1024,16]{1,2,0:T(8,128)(2,1)}, u32[]{:S(2)}) copy-start(bf16[2,1024,16]{1,2,0:T(8,128)(2,1)} %get-tuple-element.1030) | copy-start | bytes 196612 | tf_op jit(solution)/shard_map/while
  1970.9 0.7 copy-start.3
  1970.9 0.7 copy-start.6
Sparse Core Ops, SparseCore 0:
  27.2 188.2 all-reduce.5
  334.5 182.2 all-reduce.5
  635.8 182.2 all-reduce.5
  937.1 182.2 all-reduce.5
  1239.0 132.2 reduce-scatter.1
  1488.0 132.9 reduce-scatter.1
  1737.9 133.2 reduce-scatter.1
where the time goes:
time: 1980 us
  waiting for transfers between devices  1140 us (58%)
  blocking collectives  647 us (33%)
  matrix products  81.9 us (4%)
  other arithmetic  48.2 us (2%)
  local copies, waits for them, and re-layouts  26.1 us (1%)
    while x11, waiting for transfers between devices  731 us
    reduce_scatter x3, waiting for transfers between devices, solve(): share = lax.psum_scatter(summed, 'front', scatter_dimension=2, tiled=True)  399 us
    all_gather x7, blocking collectives, solve(): lax.all_gather((sep_side - share).astype(jnp.bfloat16), 'front', axis=2,...  350 us
    all_gather x7, blocking collectives, solve(): lax.all_gather(sep_sol.astype(jnp.bfloat16), 'front', axis=2, tiled=True)  297 us
  transfers between devices with their start and end apart: 14, of which 14 were waited for; matrix products, arithmetic and copies ran while one was open for 0% of the time, Pallas kernels for 0%

commit v1 on v0

v1 whole, which is shorter than its diff:
```python
import jax
import jax.numpy as jnp
from jax import lax
from jax.experimental import pallas as pl
from jax.experimental.pallas import tpu as pltpu
from jax.sharding import PartitionSpec as P

MESH = pl.DeviceIdType.MESH
F32 = jnp.float32
BF16 = jnp.bfloat16
FACE = 128
CELLS = 1280
SEP = 1024
BLOCK = 256
NT = (((1,), (1,)), ((), ()))
TN = (((0,), (0,)), ((), ()))

T_F, O_F, D_F, O_B, D_FF, T_B, D_B = range(7)
X_SINV, X_IDX, X_BASE, X_MAT, X_PART, X_SOL, X_YF, X_YB, X_FINAL, X_COUNT = 0, 1, 2, 3, 10, 13, 16, 17, 18, 19


def dot(a, b):
    return jnp.dot(a, b, preferred_element_type=F32)


def kernel(rhs_ref, bs_ref, inv_hbm, cc_ref, idx_ref, sinv_hbm, out_ref, sep_ref,
           inv, w, gm, gs, gi, pt, stage, kb, pbuf, sbuf, yout, yin, fstage, fk, accl, accf, stot, lsem, ssem, rsem):
    p = lax.axis_index("panel")
    front = lax.axis_index("front")
    x, z, c = front // 16, lax.rem(front // 2, 8), lax.rem(front, 2)
    g = x * 2 + c
    first_panel, last_panel = p == 0, p == 3

    def z_peer(k):
        other = lax.rem(z + k, 8)
        return other, (p, (x * 8 + other) * 2 + c)

    def g_peer(k):
        other = lax.rem(g + k, 8)
        return other, (p, ((other // 2) * 8 + z) * 2 + lax.rem(other, 2))

    for block in range(5):
        rows = pl.ds(block * BLOCK, BLOCK)
        pltpu.make_async_copy(inv_hbm.at[:, rows], inv.at[:, rows], lsem.at[block]).start()
    own_sinv = pltpu.make_async_copy(sinv_hbm, gs.at[:, z], lsem.at[5])
    own_sinv.start()

    barrier = pltpu.get_barrier_semaphore()
    for k in range(1, 8):
        pl.semaphore_signal(barrier, inc=1, device_id=z_peer(k)[1], device_id_type=MESH)
        pl.semaphore_signal(barrier, inc=1, device_id=g_peer(k)[1], device_id_type=MESH)

    @pl.when(p > 0)
    def _():
        pl.semaphore_signal(barrier, inc=1, device_id=(p - 1, front), device_id_type=MESH)

    @pl.when(p < 3)
    def _():
        pl.semaphore_signal(barrier, inc=1, device_id=(p + 1, front), device_id_type=MESH)

    pl.semaphore_wait(barrier, 14 + (p > 0).astype(jnp.int32) + (p < 3).astype(jnp.int32))

    def send(src, dst, which, device):
        pltpu.make_async_remote_copy(
            src_ref=src, dst_ref=dst, send_sem=ssem.at[which], recv_sem=rsem.at[which], device_id=device, device_id_type=MESH
        ).start()

    def send_z(src, dst, which):
        for k in range(1, 8):
            send(src, dst, which, z_peer(k)[1])

    def send_g(src, dst, which):
        for k in range(1, 8):
            send(src, dst, which, g_peer(k)[1])

    def wait(ref, sem):
        pltpu.make_async_copy(ref, ref, sem).wait()

    send_z(sinv_hbm, gs.at[:, z], X_SINV)
    gi[z] = idx_ref[...]
    send_z(idx_ref, gi.at[z], X_IDX)

    flat = rhs_ref[...].reshape(64, CELLS).astype(BF16)
    towards = jnp.zeros((64, 2 * FACE), F32)
    faces = [jnp.zeros((64, 2 * FACE), F32) for _ in range(2)]
    outs = [jnp.zeros((2 * FACE, 2 * FACE), F32) for _ in range(2)]
    link = jnp.concatenate([cc_ref[0], cc_ref[1]], axis=1)
    for block in range(5):
        rows = pl.ds(block * BLOCK, BLOCK)
        pltpu.make_async_copy(inv_hbm.at[:, rows], inv.at[:, rows], lsem.at[block]).wait()
        real = dot(inv[0, rows], link)
        imag = dot(inv[1, rows], link)
        part = jnp.concatenate(
            [real[:, :FACE] - imag[:, FACE:], real[:, FACE:] + imag[:, :FACE]], axis=1
        ).astype(BF16)
        w[rows] = part
        some = flat[:, block * BLOCK : (block + 1) * BLOCK]
        towards = towards + dot(some, part)
        link_rows = link[block * BLOCK : (block + 1) * BLOCK]
        for side, start in enumerate((0, CELLS - FACE)):
            cols = pl.ds(start, FACE)
            both = jnp.concatenate([inv[0, rows, cols], inv[1, rows, cols]], axis=1)
            faces[side] = faces[side] + dot(some, both)
            outs[side] = outs[side] + lax.dot_general(link_rows, both, TN, preferred_element_type=F32)

    def combine(value):
        return jnp.concatenate(
            [value[:32, :FACE] - value[32:, FACE:], value[32:, :FACE] + value[:32, FACE:]], axis=0
        )

    pieces = [combine(towards), bs_ref[...].reshape(64, FACE), combine(faces[0]), combine(faces[1])]
    for other in range(8):
        for item, value in enumerate(pieces):
            stage[other, item] = jnp.concatenate(
                [value[4 * other : 4 * other + 4], value[32 + 4 * other : 36 + 4 * other]], axis=0
            )
    for k in range(1, 8):
        other, device = z_peer(k)
        send(stage.at[other], kb.at[z], X_BASE, device)
    kb[z] = stage[z]

    for side, slot in ((0, O_B), (1, O_F)):
        value = outs[side]
        gm[slot, z] = jnp.concatenate(
            [value[:FACE, :FACE] - value[FACE:, FACE:], value[:FACE, FACE:] + value[FACE:, :FACE]], axis=1
        ).astype(BF16)
    low, high = pl.ds(0, FACE), pl.ds(CELLS - FACE, FACE)
    gm[T_F, z] = w[low]
    gm[T_B, z] = w[high]
    for slot, r, q in ((D_F, low, high), (D_FF, low, low), (D_B, high, low)):
        gm[slot, z] = jnp.concatenate([inv[0, r, q], inv[1, r, q]], axis=1)

    needed = {
        T_F: p > 0, O_F: p < 3, D_F: (p > 0) & (p < 3), O_B: p > 0, D_FF: p > 0, T_B: p < 3, D_B: (p > 0) & (p < 3)
    }
    for slot in range(7):
        @pl.when(needed[slot])
        def _(slot=slot):
            send_z(gm.at[slot, z], gm.at[slot, z], X_MAT + slot)

    def arrived(slot):
        wait(gm.at[slot, pl.ds(0, 7)], rsem.at[X_MAT + slot])

    wait(gi.at[pl.ds(0, 7)], rsem.at[X_IDX])
    unknown = lax.broadcasted_iota(jnp.int32, (SEP, FACE), 0)
    for leaf in range(8):
        row = gi[leaf][0:1, :]
        pt[:, leaf * FACE : (leaf + 1) * FACE] = jnp.where(unknown == row, 1.0, 0.0).astype(BF16)

    sign = jnp.where(lax.broadcasted_iota(jnp.int32, (8, SEP), 0) < 4, -1.0, 1.0)

    def leafwise(vector, slot):
        parts = [dot(vector[:, leaf * FACE : (leaf + 1) * FACE], gm[slot, leaf]) for leaf in range(8)]
        direct = jnp.concatenate([v[:, :FACE] for v in parts], axis=1)
        crossed = jnp.concatenate([v[:, FACE:] for v in parts], axis=1)
        return direct + sign * jnp.roll(crossed, 4, axis=0)

    def fold(value):
        half = value.shape[1] // 2
        return jnp.concatenate([value[:, :half], value[:, half:]], axis=0).astype(BF16)

    def unfold(value):
        value = value.astype(F32)
        return jnp.concatenate([value[:8], value[8:]], axis=1)

    def scatter(value):
        return lax.dot_general(value.astype(BF16), pt[...], NT, preferred_element_type=F32)

    def share(partial, turn):
        pbuf[turn, g] = fold(partial)
        send_g(pbuf.at[turn, g], pbuf.at[turn, g], X_PART + turn)

    def solve(turn):
        wait(pbuf.at[turn, pl.ds(0, 7)], rsem.at[X_PART + turn])
        total = pbuf[turn, 0].astype(F32)
        for other in range(1, 8):
            total = total + pbuf[turn, other].astype(F32)
        reduced = unfold(total).astype(BF16)
        both = lax.dot_general(reduced, gs[...].reshape(2 * FACE, SEP), NT, preferred_element_type=F32)
        mine = both[:, :FACE] + sign[:, :FACE] * jnp.roll(both[:, FACE:], 4, axis=0)
        sbuf[turn, g] = mine
        send_g(sbuf.at[turn, g], sbuf.at[turn, g], X_SOL + turn)
        wait(sbuf.at[turn, pl.ds(0, 7)], rsem.at[X_SOL + turn])
        return jnp.concatenate([sbuf[turn, other] for other in range(8)], axis=1)

    def gather(value):
        return dot(value.astype(BF16), pt[...])

    wait(kb.at[pl.ds(0, 7)], rsem.at[X_BASE])
    own = -scatter(jnp.concatenate([kb[leaf, 0] for leaf in range(8)], axis=1))
    given = kb[0, 1]
    for leaf in range(1, 8):
        given = given + kb[leaf, 1]
    own = own + jnp.concatenate([jnp.where(g == other, given, 0.0) for other in range(8)], axis=1)
    share(own, 0)
    accf[...] = jnp.concatenate([kb[leaf, 2] for leaf in range(8)], axis=1)
    accl[...] = jnp.concatenate([kb[leaf, 3] for leaf in range(8)], axis=1)
    for turn in range(2):
        @pl.when(first_panel if turn == 0 else last_panel)
        def _(turn=turn):
            yin[turn] = jnp.zeros((16, SEP // 2), BF16)

    wait(gs.at[:, pl.ds(0, 7)], rsem.at[X_SINV])
    own_sinv.wait()
    stot[...] = solve(0)

    @pl.when(p > 0)
    def _():
        wait(yin.at[0], rsem.at[X_YF])
        face = unfold(yin[0]).astype(BF16)
        arrived(T_F)
        share(-scatter(leafwise(face, T_F)), 1)
        arrived(D_FF)
        accf[...] += leafwise(face, D_FF)

        @pl.when(p < 3)
        def _():
            arrived(D_F)
            accl[...] += leafwise(face, D_F)

        stot[...] += solve(1)

    @pl.when(p < 3)
    def _():
        arrived(O_F)
        yout[0] = fold(accl[...] - leafwise(gather(stot[...]).astype(BF16), O_F))
        send(yout.at[0], yin.at[0], X_YF, (p + 1, front))

    @pl.when(p < 3)
    def _():
        wait(yin.at[1], rsem.at[X_YB])
        face = unfold(yin[1]).astype(BF16)
        arrived(T_B)
        share(-scatter(leafwise(face, T_B)), 2)

        @pl.when(p > 0)
        def _():
            arrived(D_B)
            accf[...] += leafwise(face, D_B)

        stot[...] += solve(2)

    picked = gather(stot[...])

    @pl.when(p > 0)
    def _():
        arrived(O_B)
        yout[1] = fold(accf[...] - leafwise(picked.astype(BF16), O_B))
        send(yout.at[1], yin.at[1], X_YB, (p - 1, front))

    low_face, high_face = unfold(yin[0]), unfold(yin[1])
    own_sep = sbuf[0, g]
    own_sep = own_sep + jnp.where(p > 0, sbuf[1, g], 0.0)
    own_sep = own_sep + jnp.where(p < 3, sbuf[2, g], 0.0)
    for leaf in range(8):
        cols = slice(leaf * FACE, (leaf + 1) * FACE)
        fstage[leaf, 0] = picked[:, cols]
        fstage[leaf, 1] = low_face[:, cols]
        fstage[leaf, 2] = high_face[:, cols]
        fstage[leaf, 3] = own_sep
    for k in range(1, 8):
        other, device = z_peer(k)
        send(fstage.at[other], fk.at[z], X_FINAL, device)
    fk[z] = fstage[z]
    wait(fk.at[pl.ds(0, 7)], rsem.at[X_FINAL])
    sep_ref[...] = jnp.concatenate([fk[other, 3:4] for other in range(8)], axis=0)

    def rows_of(item):
        tops = [fk[other, item][:4] for other in range(8)]
        bottoms = [fk[other, item][4:] for other in range(8)]
        return jnp.concatenate(tops, axis=0), jnp.concatenate(bottoms, axis=0)

    pick_re, pick_im = rows_of(0)
    doubled = jnp.concatenate(
        [jnp.concatenate([pick_re, -pick_im], axis=1), jnp.concatenate([pick_im, pick_re], axis=1)], axis=0
    ).astype(BF16)
    side = rhs_ref[...].reshape(64, CELLS) - lax.dot_general(doubled, link, NT, preferred_element_type=F32)
    add_low = jnp.concatenate(rows_of(1), axis=0)
    add_high = jnp.concatenate(rows_of(2), axis=0)
    side = jnp.concatenate(
        [side[:, :FACE] + add_low, side[:, FACE : CELLS - FACE], side[:, CELLS - FACE :] + add_high], axis=1
    ).astype(BF16)
    for block in range(5):
        cols = pl.ds(block * BLOCK, BLOCK)
        real = dot(side, inv[0, :, cols])
        imag = dot(side, inv[1, :, cols])
        out_ref[0, :, cols] = real[:32] - imag[32:]
        out_ref[1, :, cols] = real[32:] + imag[:32]

    def left(ref, which):
        wait(ref, ssem.at[which])

    left(gs.at[:, pl.ds(0, 7)], X_SINV)
    left(gi.at[pl.ds(0, 7)], X_IDX)
    left(kb.at[pl.ds(0, 7)], X_BASE)
    left(fk.at[pl.ds(0, 7)], X_FINAL)
    for slot in range(7):
        @pl.when(needed[slot])
        def _(slot=slot):
            left(gm.at[slot, pl.ds(0, 7)], X_MAT + slot)
    for turn, used in ((0, None), (1, p > 0), (2, p < 3)):
        def both_left(turn=turn):
            left(pbuf.at[turn, pl.ds(0, 7)], X_PART + turn)
            left(sbuf.at[turn, pl.ds(0, 7)], X_SOL + turn)
        if used is None:
            both_left()
        else:
            pl.when(used)(both_left)

    @pl.when(p < 3)
    def _():
        left(yin.at[0], X_YF)

    @pl.when(p > 0)
    def _():
        left(yin.at[1], X_YB)


def local(leaf_rhs, sep_rhs, leaf_inverse, coupling, sep_index, sep_inverse):
    z = lax.rem(lax.axis_index("front") // 2, 8)
    t = sep_index[0, 0]
    order = ((t // 256) * 2 + (t // 16) % 2) * 128 + ((t // 32) % 8) * 16 + t % 16
    index = jnp.broadcast_to(order[None, :], (8, FACE))
    sinv = sep_inverse[0].reshape(2, 4, 8, 2, 16, 16).transpose(0, 5, 1, 3, 2, 4).reshape(2, 16, SEP)
    lane = lax.broadcasted_iota(jnp.int32, (1, 1, FACE), 2)
    given = jnp.where(lane // 16 == z, jnp.tile(sep_rhs[0], (1, 1, 8)), 0.0)
    vmem = pl.BlockSpec(memory_space=pltpu.VMEM)
    hbm = pl.BlockSpec(memory_space=pl.ANY)
    leaf, sep = pl.pallas_call(
        kernel,
        out_shape=(jax.ShapeDtypeStruct((2, 32, CELLS), F32), jax.ShapeDtypeStruct((8, 8, FACE), F32)),
        in_specs=[vmem, vmem, hbm, vmem, vmem, hbm],
        out_specs=(vmem, vmem),
        scratch_shapes=[
            pltpu.VMEM((2, CELLS, CELLS), BF16),
            pltpu.VMEM((CELLS, 2 * FACE), BF16),
            pltpu.VMEM((7, 8, FACE, 2 * FACE), BF16),
            pltpu.VMEM((2, 8, 16, SEP), BF16),
            pltpu.VMEM((8, 8, FACE), jnp.int32),
            pltpu.VMEM((SEP, SEP), BF16),
            pltpu.VMEM((8, 4, 8, FACE), F32),
            pltpu.VMEM((8, 4, 8, FACE), F32),
            pltpu.VMEM((3, 8, 16, SEP // 2), BF16),
            pltpu.VMEM((3, 8, 8, FACE), F32),
            pltpu.VMEM((2, 16, SEP // 2), BF16),
            pltpu.VMEM((2, 16, SEP // 2), BF16),
            pltpu.VMEM((8, 4, 8, FACE), F32),
            pltpu.VMEM((8, 4, 8, FACE), F32),
            pltpu.VMEM((8, SEP), F32),
            pltpu.VMEM((8, SEP), F32),
            pltpu.VMEM((8, SEP), F32),
            pltpu.SemaphoreType.DMA((6,)),
            pltpu.SemaphoreType.DMA((X_COUNT,)),
            pltpu.SemaphoreType.DMA((X_COUNT,)),
        ],
        compiler_params=pltpu.CompilerParams(
            collective_id=0, has_side_effects=True, vmem_limit_bytes=48 * 2**20
        ),
    )(leaf_rhs[0, 0], given, leaf_inverse[0, 0], coupling[0, 0], index, sinv)
    mine = lax.dynamic_slice_in_dim(sep, z * 16, 16, axis=2)
    sep_out = mine.reshape(8, 2, 4, 16).transpose(1, 0, 2, 3).reshape(2, 32, 16)
    return leaf[None, None], sep_out[None]


def solution(mesh):
    in_specs = (
        P("panel", "front", None, None, None),
        P("panel", None, None, "front"),
        P("panel", "front", None, None, None),
        P("panel", "front", None, None, None),
        P("panel", "front", None),
        P("panel", None, None, "front"),
    )
    out_specs = (P("panel", "front", None, None, None), P("panel", None, None, "front"))
    return jax.shard_map(local, mesh=mesh, in_specs=in_specs, out_specs=out_specs, check_vma=False)
```

time: 1980 us -> 164 us (0.08)
  waiting for transfers between devices: 1140 us -> 0 us
  blocking collectives: 647 us -> 0 us
  Pallas kernels: 0 us -> 156 us
  matrix products: 81.9 us -> 0 us
  other arithmetic: 48.2 us -> 0.7 us
    while x11 -> x0, waiting for transfers between devices: 731 us -> none
    all_gather x14 -> x0, blocking collectives: 647 us -> none  [the longest x7 350 us: solve(): lax.all_gather((sep_side - share).astype(jnp.bfloat16), 'front', axis=2,...]
    reduce_scatter x3 -> x0, waiting for transfers between devices: 399 us -> none  [solve(): share = lax.psum_scatter(summed, 'front', scatter_dimension=2, tiled=True)]
    pallas_call x0 -> x1, Pallas kernels: none -> 156 us  [local(): pl.pallas_call(kernel, out_shape=(jax.ShapeDtypeStruct((2, 32, CELLS), F3...]
    dot_general x70 -> x0, matrix products: 81.9 us -> none  [the longest x28 39.3 us: complex_rows(): real_part = jnp.dot(flat, matrix[0], preferred_element_type=jnp.float32)]
    scatter-add x11 -> x0, other arithmetic: 34.5 us -> none  [the longest x7 34.5 us: solve(): jnp.zeros((2, rows_group, sep_whole), jnp.float32).at[:, :, index]]
  transfers between devices with their start and end apart: 14 -> 0, of which waited for: 14 -> 0; matrix products, arithmetic and copies ran while one was open for 0% -> 0% of each run, Pallas kernels for 0% -> 0%
where the time goes in v1:
time: 164 us
  Pallas kernels  156 us (95%)
  local copies, waits for them, and re-layouts  6.47 us (4%)
    pallas_call x1, Pallas kernels, local(): pl.pallas_call(kernel, out_shape=(jax.ShapeDtypeStruct((2, 32, CELLS), F3...  156 us
    unnamed x6, local copies, waits for them, and re-layouts  3.46 us

profile of v1, /device:TPU:1, one launch (start us, length us, event | category | flops | bytes accessed | tf_op | source)
XLA Modules:
  0.0 163.5 jit_solution(6293722017309782995)
XLA Ops:
  0.7 0.7 tile.11
  1.4 0.1 copy.10
  1.5 1.2 reshape_squeeze.3
  2.7 0.1 copy.16
  2.9 0.8 reshape.149.sinv_hbm
  3.6 0.7 fusion.1
  4.3 0.0 copy-start
  4.3 1.1 copy-done
  5.4 0.0 copy-start.1
  5.4 1.0 copy-done.1
  6.4 155.6 %shard_map.77 = (f32[2,32,1280]{2,1,0:T(8,128)S(1)}, f32[8,8,128]{2,1,0:T(8,128)S(1)}) custom-call(f32[2,32,1280]{2,1,0:T(8,128)S(1)} %bitcast.38, f32[2,32,128]{2,1,0:T(8,128)S(1)} %broadcast_select_fusion.bs_ref, bf16[2,1280,1280]{2,1,0:T(8,128)(2,1)} %bitcast.40, bf16[2,1280,128]{2,1,0:T(8,128)(2,1)S(1)} %bitcast.37, ...), custom_call_target="tpu_custom_call" | custom-call | tf_op jit(solution)/shard_map/pallas_call | solution.py:329
  162.0 0.1 constant_dynamic-slice_fusion
  162.1 0.7 copy.14
  162.8 0.7 copy.18
  (5 shorter events, 0.0 us)
Async XLA Ops:
  4.3 1.1 copy-start
  5.4 1.0 copy-start.1

commit v2 on v1

v2 whole, which is shorter than its diff:
```python
import jax
import jax.numpy as jnp
from jax import lax
from jax.experimental import pallas as pl
from jax.experimental.pallas import tpu as pltpu
from jax.sharding import PartitionSpec as P

MESH = pl.DeviceIdType.MESH
F32 = jnp.float32
BF16 = jnp.bfloat16
FACE = 128
CELLS = 1280
SEP = 1024
BLOCK = 256
NT = (((1,), (1,)), ((), ()))
TN = (((0,), (0,)), ((), ()))

S_T, S_O, S_D, S_O2, S_T2, S_D2, S_DFF, R_SINV = range(8)
FIRST_SET, SECOND_SET = (S_O, S_T, S_D), (S_O2, S_T2, S_D2, S_DFF)
X_UP, X_DOWN, X_IDX, X_BASE, X_T, X_T2, X_PART, X_SOL, X_Y, X_FINAL, X_COUNT = 0, 1, 2, 3, 4, 5, 6, 9, 12, 15, 16


def dot(a, b):
    return jnp.dot(a, b, preferred_element_type=F32)


def kernel(rhs_hbm, bs_hbm, inv_hbm, cc_hbm, idx_hbm, sinv_hbm, out_ref, sep_ref,
           rhs, bs, inv, cc, idx, w, tst, gm, gs, gi, pto, ptb, pta, ptz, stage, kb, pbuf, pout, sbuf, yout, yin,
           bst, fstage, fk, acca, accb, stot, lsem, ssem, rsem, rs, rr):
    p = lax.axis_index("panel")
    front = lax.axis_index("front")
    x, z, c = front // 16, lax.rem(front // 2, 8), lax.rem(front, 2)
    g = x * 2 + c
    middle = (p > 0) & (p < 3)
    ahead = jnp.where(p < 3, p + 1, 2)
    turn_ahead = jnp.where(p < 3, 1, 2)

    def z_peer(k):
        other = lax.rem(z + k, 8)
        return other, (p, (x * 8 + other) * 2 + c)

    def g_peer(k, panel):
        other = lax.rem(g + k, 8)
        return panel, ((other // 2) * 8 + z) * 2 + lax.rem(other, 2)

    def load(src, dst, number):
        copy = pltpu.make_async_copy(src, dst, lsem.at[number])
        copy.start()
        return copy

    load_sinv = load(sinv_hbm, gs.at[:, z], 0)
    load_idx = load(idx_hbm, idx, 1)
    load_cc = load(cc_hbm, cc, 2)
    load_inv = []
    for block in range(5):
        rows = pl.ds(block * BLOCK, BLOCK)
        load_inv.append(load(inv_hbm.at[:, rows], inv.at[:, rows], 3 + block))
        if block == 0:
            load_rhs = load(rhs_hbm, rhs, 8)
    load_bs = load(bs_hbm, bs, 9)

    barrier = pltpu.get_barrier_semaphore()

    def greet(device):
        pl.semaphore_signal(barrier, inc=1, device_id=device, device_id_type=MESH)

    for k in range(1, 8):
        greet(z_peer(k)[1])
        greet(g_peer(k, p))

    @pl.when(p > 0)
    def _():
        for k in range(8):
            greet(g_peer(k, p - 1))

    @pl.when(p < 3)
    def _():
        for k in range(8):
            greet(g_peer(k, p + 1))

    bst[...] = jnp.zeros((2, FACE, 32), F32)
    pl.semaphore_wait(barrier, 14 + jnp.where(p > 0, 8, 0) + jnp.where(p < 3, 8, 0))

    def send(src, dst, which, device):
        pltpu.make_async_remote_copy(
            src_ref=src, dst_ref=dst, send_sem=ssem.at[which], recv_sem=rsem.at[which], device_id=device, device_id_type=MESH
        ).start()

    def wait(ref, sem):
        pltpu.make_async_copy(ref, ref, sem).wait()

    def block_of(slot, owner):
        return gs.at[:, owner] if slot == R_SINV else gm.at[slot, owner]

    def ring(slot, step):
        for way, steps in ((0, 4), (1, 3)):
            if step < steps:
                if step > 0:
                    wait(block_of(slot, 0), rr.at[slot, way, step - 1])
                owner = lax.rem(z + (8 - step if way == 0 else step), 8)
                pltpu.make_async_remote_copy(
                    src_ref=block_of(slot, owner), dst_ref=block_of(slot, owner), send_sem=rs.at[slot, way, step],
                    recv_sem=rr.at[slot, way, step], device_id=z_peer(1 if way == 0 else 7)[1], device_id_type=MESH
                ).start()

    def ring_end(slot):
        wait(block_of(slot, 0), rr.at[slot, 0, 3])
        wait(block_of(slot, 0), rr.at[slot, 1, 2])

    def ring_left(slot):
        for way, steps in ((0, 4), (1, 3)):
            for step in range(steps):
                wait(block_of(slot, 0), rs.at[slot, way, step])

    def first_set(step):
        ring(S_O, step)
        ring(S_T, step)

        @pl.when(p > 0)
        def _():
            ring(S_D, step)

    def second_set(step):
        for slot in SECOND_SET:
            ring(slot, step)

    load_sinv.wait()
    ring(R_SINV, 0)
    load_idx.wait()
    own_index = jnp.broadcast_to(idx[...], (8, FACE))
    gi[z, 0] = own_index

    @pl.when(p == 0)
    def _():
        gi[z, 2] = own_index

    @pl.when(p == 3)
    def _():
        gi[z, 1] = own_index

    @pl.when(p < 3)
    def _():
        send(gi.at[z, 0], gi.at[z, 2], X_UP, (p + 1, front))

    @pl.when(p > 0)
    def _():
        send(gi.at[z, 0], gi.at[z, 1], X_DOWN, (p - 1, front))

    load_cc.wait()
    load_rhs.wait()
    flat = rhs[...].reshape(64, CELLS).astype(BF16)
    towards = jnp.zeros((64, 2 * FACE), F32)
    faces = [jnp.zeros((64, 2 * FACE), F32) for _ in range(2)]
    link = jnp.concatenate([cc[0], cc[1]], axis=1)
    starts = (0, CELLS - FACE)
    for block in range(5):
        rows = pl.ds(block * BLOCK, BLOCK)
        load_inv[block].wait()
        real = dot(inv[0, rows], link)
        imag = dot(inv[1, rows], link)
        part = jnp.concatenate(
            [real[:, :FACE] - imag[:, FACE:], real[:, FACE:] + imag[:, :FACE]], axis=1
        ).astype(BF16)
        w[rows] = part
        some = flat[:, block * BLOCK : (block + 1) * BLOCK]
        towards = towards + dot(some, part)
        for side, start in enumerate(starts):
            cols = pl.ds(start, FACE)
            both = jnp.concatenate([inv[0, rows, cols], inv[1, rows, cols]], axis=1)
            faces[side] = faces[side] + dot(some, both)
        if block == 0:
            tst[0] = part[:FACE]

            @pl.when(p > 0)
            def _():
                send(tst.at[0], gm.at[S_T, z], X_T, (p - 1, front))
        if block == 1:
            ring(R_SINV, 1)

            @pl.when(p > 0)
            def _():
                wait(gi.at[0, 0], rsem.at[X_UP])

            @pl.when(p < 3)
            def _():
                wait(gi.at[0, 0], rsem.at[X_DOWN])

            for k in range(1, 8):
                send(gi.at[z], gi.at[z], X_IDX, z_peer(k)[1])
        if block == 3:
            ring(R_SINV, 2)
    tst[1] = w[pl.ds(CELLS - FACE, FACE)]

    def combine(value):
        return jnp.concatenate(
            [value[:32, :FACE] - value[32:, FACE:], value[32:, :FACE] + value[:32, FACE:]], axis=0
        )

    load_bs.wait()
    place = pl.ds(pl.multiple_of(lax.rem(z, 4) * 32 + c * 16, 16), 16)
    for part in range(2):
        bst[part, place] = bs[part]
    given = jnp.concatenate([jnp.transpose(bst[0]), jnp.transpose(bst[1])], axis=0)
    face_first, face_last = combine(faces[0]), combine(faces[1])
    pieces = [combine(towards), given, jnp.where(p < 3, face_last, face_first), face_first]
    for other in range(8):
        for item, value in enumerate(pieces):
            stage[other, item] = jnp.concatenate(
                [value[4 * other : 4 * other + 4], value[32 + 4 * other : 36 + 4 * other]], axis=0
            )
    for k in range(1, 8):
        other, device = z_peer(k)
        send(stage.at[other], kb.at[z], X_BASE, device)
    kb[z] = stage[z]

    @pl.when(p == 2)
    def _():
        send(tst.at[1], gm.at[S_T, z], X_T, (3, front))

    @pl.when(p < 2)
    def _():
        send(tst.at[1], gm.at[S_T2, z], X_T2, (p + 1, front))

    ring(R_SINV, 3)
    outs = []
    for side, start in enumerate(starts):
        total = jnp.zeros((2 * FACE, 2 * FACE), F32)
        for block in range(5):
            rows, cols = pl.ds(block * BLOCK, BLOCK), pl.ds(start, FACE)
            both = jnp.concatenate([inv[0, rows, cols], inv[1, rows, cols]], axis=1)
            total = total + lax.dot_general(
                link[block * BLOCK : (block + 1) * BLOCK], both, TN, preferred_element_type=F32
            )
        outs.append(
            jnp.concatenate(
                [total[:FACE, :FACE] - total[FACE:, FACE:], total[:FACE, FACE:] + total[FACE:, :FACE]], axis=1
            )
        )
    gm[S_O, z] = jnp.where(p < 3, outs[1], outs[0]).astype(BF16)
    gm[S_O2, z] = outs[0].astype(BF16)
    low, high = pl.ds(0, FACE), pl.ds(CELLS - FACE, FACE)
    d_ff = jnp.concatenate([inv[0, low, low], inv[1, low, low]], axis=1)
    gm[S_DFF, z] = d_ff
    gm[S_D2, z] = jnp.concatenate([inv[0, high, low], inv[1, high, low]], axis=1)
    gm[S_D, z] = jnp.where(p < 3, jnp.concatenate([inv[0, low, high], inv[1, low, high]], axis=1), d_ff)
    wait(gm.at[S_T, 0], rsem.at[X_T])
    first_set(0)

    unknown = lax.broadcasted_iota(jnp.int32, (SEP, FACE), 0)

    def select(dst, item, by_row=False):
        for leaf in range(8):
            row = gi[leaf, item][0:1, :]
            if by_row:
                row = ((row >> 8) * 2 + ((row >> 4) & 1)) * 128 + ((row >> 5) & 7) * 16 + (row & 15)
            dst[:, leaf * FACE : (leaf + 1) * FACE] = jnp.where(unknown == row, 1.0, 0.0).astype(BF16)

    wait(gi.at[pl.ds(0, 7)], rsem.at[X_IDX])
    select(ptb, 0)

    sign = jnp.where(lax.broadcasted_iota(jnp.int32, (8, SEP), 0) < 4, -1.0, 1.0)

    def leafwise(vector, slot):
        parts = [dot(vector[:, leaf * FACE : (leaf + 1) * FACE], gm[slot, leaf]) for leaf in range(8)]
        direct = jnp.concatenate([v[:, :FACE] for v in parts], axis=1)
        crossed = jnp.concatenate([v[:, FACE:] for v in parts], axis=1)
        return direct + sign * jnp.roll(crossed, 4, axis=0)

    def fold(value):
        half = value.shape[1] // 2
        return jnp.concatenate([value[:, :half], value[:, half:]], axis=0).astype(BF16)

    def unfold(value):
        value = value.astype(F32)
        return jnp.concatenate([value[:8], value[8:]], axis=1)

    def scatter(value, matrix):
        return lax.dot_general(value.astype(BF16), matrix[...], NT, preferred_element_type=F32)

    def gather(value):
        return dot(value.astype(BF16), pto[...])

    def solve(turn, arrived, before, meanwhile):
        before()
        wait(pbuf.at[turn, pl.ds(0, arrived)], rsem.at[X_PART + turn])
        total = pbuf[turn, 0].astype(F32)
        for other in range(1, 8):
            total = total + pbuf[turn, other].astype(F32)
        reduced = unfold(total).astype(BF16)
        both = lax.dot_general(reduced, gs[...].reshape(2 * FACE, SEP), NT, preferred_element_type=F32)
        mine = both[:, :FACE] + sign[:, :FACE] * jnp.roll(both[:, FACE:], 4, axis=0)
        sbuf[turn, g] = mine
        for k in range(1, 8):
            send(sbuf.at[turn, g], sbuf.at[turn, g], X_SOL + turn, g_peer(k, p))
        meanwhile()
        wait(sbuf.at[turn, pl.ds(0, 7)], rsem.at[X_SOL + turn])
        return jnp.concatenate([sbuf[turn, other] for other in range(8)], axis=1)

    def onward(face, matrix, slot, which, turn, panel):
        face_low = face.astype(BF16)
        pout[which] = fold(-scatter(leafwise(face_low, slot), matrix))
        for k in range(8):
            send(pout.at[which], pbuf.at[turn, g], X_PART + turn, g_peer(k, panel))
        yout[which] = fold(face)
        send(yout.at[which], yin.at[turn], X_Y + turn, (panel, front))

    wait(kb.at[pl.ds(0, 7)], rsem.at[X_BASE])
    own = -scatter(jnp.concatenate([kb[leaf, 0] for leaf in range(8)], axis=1), ptb)
    given_low = (kb[0, 1] + kb[1, 1]) + (kb[2, 1] + kb[3, 1])
    given_high = (kb[4, 1] + kb[5, 1]) + (kb[6, 1] + kb[7, 1])
    own = own + jnp.concatenate(
        [jnp.where(x == other // 2, given_low if other % 2 == 0 else given_high, 0.0) for other in range(8)], axis=1
    )
    pbuf[0, g] = fold(own)
    for k in range(1, 8):
        send(pbuf.at[0, g], pbuf.at[0, g], X_PART, g_peer(k, p))
    acca[...] = jnp.concatenate([kb[leaf, 2] for leaf in range(8)], axis=1)
    accb[...] = jnp.concatenate([kb[leaf, 3] for leaf in range(8)], axis=1)

    @pl.when(p == 0)
    def _():
        yin[1] = jnp.zeros((16, SEP // 2), BF16)

    @pl.when(p == 3)
    def _():
        yin[2] = jnp.zeros((16, SEP // 2), BF16)

    def base_before():
        select(pto, 0, by_row=True)
        first_set(1)
        ring_end(R_SINV)

    def base_meanwhile():
        @pl.when(p < 3)
        def _():
            select(pta, 1)

        @pl.when(p == 3)
        def _():
            select(pta, 2)

        first_set(2)

    stot[...] = solve(0, 7, base_before, base_meanwhile)
    first_set(3)

    @pl.when(middle)
    def _():
        wait(gm.at[S_T2, 0], rsem.at[X_T2])
        second_set(0)
        second_set(1)

    @pl.when(p > 0)
    def _():
        def meanwhile():
            wait(yin.at[1], rsem.at[X_Y + 1])
            ring_end(S_D)
            acca[...] += leafwise(unfold(yin[1]).astype(BF16), S_D)

        stot[...] += solve(1, 8, lambda: None, meanwhile)

    ring_end(S_O)
    ring_end(S_T)
    onward(acca[...] - leafwise(gather(stot[...]).astype(BF16), S_O), pta, S_T, 0, turn_ahead, ahead)

    @pl.when(middle)
    def _():
        select(ptz, 2)
        second_set(2)
        second_set(3)
        for slot in SECOND_SET:
            ring_end(slot)
        accb[...] += leafwise(unfold(yin[1]).astype(BF16), S_DFF)

    @pl.when(p < 3)
    def _():
        def meanwhile():
            wait(yin.at[2], rsem.at[X_Y + 2])

            @pl.when(p > 0)
            def _():
                accb[...] += leafwise(unfold(yin[2]).astype(BF16), S_D2)

        stot[...] += solve(2, 8, lambda: None, meanwhile)

    picked = gather(stot[...])

    @pl.when(middle)
    def _():
        onward(accb[...] - leafwise(picked.astype(BF16), S_O2), ptz, S_T2, 1, 2, p - 1)

    low_face, high_face = unfold(yin[1]), unfold(yin[2])
    own_sep = sbuf[0, g]
    own_sep = own_sep + jnp.where(p > 0, sbuf[1, g], 0.0)
    own_sep = own_sep + jnp.where(p < 3, sbuf[2, g], 0.0)
    for leaf in range(8):
        cols = slice(leaf * FACE, (leaf + 1) * FACE)
        fstage[leaf, 0] = picked[:, cols]
        fstage[leaf, 1] = low_face[:, cols]
        fstage[leaf, 2] = high_face[:, cols]
        fstage[leaf, 3] = own_sep
    for k in range(1, 8):
        other, device = z_peer(k)
        send(fstage.at[other], fk.at[z], X_FINAL, device)
    fk[z] = fstage[z]
    wait(fk.at[pl.ds(0, 7)], rsem.at[X_FINAL])

    def rows_of(item):
        tops = [fk[other, item][:4] for other in range(8)]
        bottoms = [fk[other, item][4:] for other in range(8)]
        return jnp.concatenate(tops, axis=0), jnp.concatenate(bottoms, axis=0)

    for part, value in enumerate(rows_of(3)):
        bst[part] = jnp.transpose(value)
        sep_ref[part] = bst[part, pl.ds(pl.multiple_of(z * 16, 16), 16)]
    pick_re, pick_im = rows_of(0)
    doubled = jnp.concatenate(
        [jnp.concatenate([pick_re, -pick_im], axis=1), jnp.concatenate([pick_im, pick_re], axis=1)], axis=0
    ).astype(BF16)
    side = rhs[...].reshape(64, CELLS) - lax.dot_general(doubled, link, NT, preferred_element_type=F32)
    add_low = jnp.concatenate(rows_of(1), axis=0)
    add_high = jnp.concatenate(rows_of(2), axis=0)
    side = jnp.concatenate(
        [side[:, :FACE] + add_low, side[:, FACE : CELLS - FACE], side[:, CELLS - FACE :] + add_high], axis=1
    ).astype(BF16)
    for block in range(5):
        cols = pl.ds(block * BLOCK, BLOCK)
        real = dot(side, inv[0, :, cols])
        imag = dot(side, inv[1, :, cols])
        out_ref[0, :, cols] = real[:32] - imag[32:]
        out_ref[1, :, cols] = real[32:] + imag[:32]

    ring_left(R_SINV)
    ring_left(S_O)
    ring_left(S_T)
    wait(gi.at[pl.ds(0, 7)], ssem.at[X_IDX])
    wait(kb.at[pl.ds(0, 7)], ssem.at[X_BASE])
    wait(fk.at[pl.ds(0, 7)], ssem.at[X_FINAL])
    wait(pbuf.at[0, pl.ds(0, 7)], ssem.at[X_PART])
    wait(sbuf.at[0, pl.ds(0, 7)], ssem.at[X_SOL])

    @pl.when(p > 0)
    def _():
        ring_left(S_D)
        wait(gi.at[0, 0], ssem.at[X_DOWN])
        wait(pbuf.at[2], ssem.at[X_PART + 2])
        wait(sbuf.at[1, pl.ds(0, 7)], ssem.at[X_SOL + 1])
        wait(yin.at[2], ssem.at[X_Y + 2])

    @pl.when(p < 3)
    def _():
        wait(gi.at[0, 0], ssem.at[X_UP])
        wait(pbuf.at[1], ssem.at[X_PART + 1])
        wait(sbuf.at[2, pl.ds(0, 7)], ssem.at[X_SOL + 2])
        wait(yin.at[1], ssem.at[X_Y + 1])

    @pl.when((p == 1) | (p == 3))
    def _():
        wait(tst.at[0], ssem.at[X_T])

    @pl.when(p == 2)
    def _():
        wait(tst, ssem.at[X_T])

    @pl.when(p < 2)
    def _():
        wait(tst.at[1], ssem.at[X_T2])

    @pl.when(middle)
    def _():
        for slot in SECOND_SET:
            ring_left(slot)


def local(leaf_rhs, sep_rhs, leaf_inverse, coupling, sep_index, sep_inverse):
    vmem = pl.BlockSpec(memory_space=pltpu.VMEM)
    hbm = pl.BlockSpec(memory_space=pl.ANY)
    leaf, sep = pl.pallas_call(
        kernel,
        out_shape=(jax.ShapeDtypeStruct((2, 32, CELLS), F32), jax.ShapeDtypeStruct((2, 16, 32), F32)),
        in_specs=[hbm] * 6,
        out_specs=(vmem, vmem),
        scratch_shapes=[
            pltpu.VMEM((2, 32, CELLS), F32),
            pltpu.VMEM((2, 16, 32), F32),
            pltpu.VMEM((2, CELLS, CELLS), BF16),
            pltpu.VMEM((2, CELLS, FACE), BF16),
            pltpu.VMEM((1, FACE), jnp.int32),
            pltpu.VMEM((CELLS, 2 * FACE), BF16),
            pltpu.VMEM((2, FACE, 2 * FACE), BF16),
            pltpu.VMEM((7, 8, FACE, 2 * FACE), BF16),
            pltpu.VMEM((2, 8, 16, SEP), BF16),
            pltpu.VMEM((8, 3, 8, FACE), jnp.int32),
            pltpu.VMEM((SEP, SEP), BF16),
            pltpu.VMEM((SEP, SEP), BF16),
            pltpu.VMEM((SEP, SEP), BF16),
            pltpu.VMEM((SEP, SEP), BF16),
            pltpu.VMEM((8, 4, 8, FACE), F32),
            pltpu.VMEM((8, 4, 8, FACE), F32),
            pltpu.VMEM((3, 8, 16, SEP // 2), BF16),
            pltpu.VMEM((2, 16, SEP // 2), BF16),
            pltpu.VMEM((3, 8, 8, FACE), F32),
            pltpu.VMEM((2, 16, SEP // 2), BF16),
            pltpu.VMEM((3, 16, SEP // 2), BF16),
            pltpu.VMEM((2, FACE, 32), F32),
            pltpu.VMEM((8, 4, 8, FACE), F32),
            pltpu.VMEM((8, 4, 8, FACE), F32),
            pltpu.VMEM((8, SEP), F32),
            pltpu.VMEM((8, SEP), F32),
            pltpu.VMEM((8, SEP), F32),
            pltpu.SemaphoreType.DMA((10,)),
            pltpu.SemaphoreType.DMA((X_COUNT,)),
            pltpu.SemaphoreType.DMA((X_COUNT,)),
            pltpu.SemaphoreType.DMA((8, 2, 4)),
            pltpu.SemaphoreType.DMA((8, 2, 4)),
        ],
        compiler_params=pltpu.CompilerParams(
            collective_id=0, has_side_effects=True, vmem_limit_bytes=56 * 2**20
        ),
    )(
        leaf_rhs[0, 0], sep_rhs[0].transpose(0, 2, 1), leaf_inverse[0, 0], coupling[0, 0], sep_index[0],
        sep_inverse[0].transpose(0, 2, 1)
    )
    return leaf[None, None], sep.transpose(0, 2, 1)[None]


def solution(mesh):
    in_specs = (
        P("panel", "front", None, None, None),
        P("panel", None, None, "front"),
        P("panel", "front", None, None, None),
        P("panel", "front", None, None, None),
        P("panel", "front", None),
        P("panel", None, None, "front"),
    )
    out_specs = (P("panel", "front", None, None, None), P("panel", None, None, "front"))
    return jax.shard_map(local, mesh=mesh, in_specs=in_specs, out_specs=out_specs, check_vma=False)
```

time: 164 us -> 113 us (0.69)
  Pallas kernels: 156 us -> 110 us
  local copies, waits for them, and re-layouts: 6.47 us -> 3.04 us
    pallas_call x1, Pallas kernels: 156 us -> 110 us  [local(): pl.pallas_call(kernel, out_shape=(jax.ShapeDtypeStruct((2, 32, CELLS), F3...]
    another operation x4 -> x0, local copies, waits for them, and re-layouts: 2.15 us -> none  [the longest x2 1.36 us: local(): sep_inverse[0].reshape(2, 4, 8, 2, 16, 16).transpose(0, 5, 1, 3, 2, 4)]
    unnamed x6 -> x2, local copies, waits for them, and re-layouts: 3.46 us -> 3.04 us
where the time goes in v2:
time: 113 us
  Pallas kernels  110 us (97%)
  local copies, waits for them, and re-layouts  3.04 us (3%)
    pallas_call x1, Pallas kernels, local(): pl.pallas_call(kernel, out_shape=(jax.ShapeDtypeStruct((2, 32, CELLS), F3...  110 us
    unnamed x2, local copies, waits for them, and re-layouts  3.04 us

profile of v2, /device:TPU:1, one launch (start us, length us, event | category | flops | bytes accessed | tf_op | source)
XLA Modules:
  0.0 113.3 jit_solution(12587912935868721752)
XLA Ops:
  0.6 109.6 %shard_map.77 = (f32[2,32,1280]{2,1,0:T(8,128)}, f32[2,16,32]{2,1,0:T(8,128)}) custom-call(f32[2,32,1280]{2,1,0:T(8,128)} %bitcast.16, f32[2,16,32]{2,1,0:T(8,128)} %bitcast.19, bf16[2,1280,1280]{2,1,0:T(8,128)(2,1)} %bitcast.14, bf16[2,1280,128]{2,1,0:T(8,128)(2,1)} %bitcast.15, s32[1,128]{1,0:T(1,128)} %bitcast.21, bf16[2,16,1024]{2,1,0:T(8,128)(2,1)} %bitcast.18), custom_call_target="tpu_custom_call" | custom-call | tf_op jit(solution)/shard_map/pallas_call | solution.py:478
  110.2 1.7 %copy.10 = f32[1,1,2,32,1280]{4,3,2,1,0:T(8,128)} copy(f32[1,1,2,32,1280]{4,3,2,1,0:T(8,128)} %bitcast.17) | data formatting | bytes 655360
  111.9 1.3 %copy.11 = f32[1,2,32,16]{2,3,1,0:T(8,128)} copy(f32[1,2,32,16]{2,3,1,0:T(8,128)} %bitcast.20) | data formatting | bytes 8192

commit v3 on v2

--- a/solution.py
+++ b/solution.py
@@ -16,8 +16,9 @@
 TN = (((0,), (0,)), ((), ()))
 
 S_T, S_O, S_D, S_O2, S_T2, S_D2, S_DFF, R_SINV = range(8)
+Z_ORDER, G_ORDER = (4, 3, 5, 2, 6, 1, 7), (4, 5, 2, 6, 3, 7, 1, 0)
 FIRST_SET, SECOND_SET = (S_O, S_T, S_D), (S_O2, S_T2, S_D2, S_DFF)
-X_UP, X_DOWN, X_IDX, X_BASE, X_T, X_T2, X_PART, X_SOL, X_Y, X_FINAL, X_COUNT = 0, 1, 2, 3, 4, 5, 6, 9, 12, 15, 16
+X_UP, X_DOWN, X_IDX, X_BASE, X_T, X_T2, X_PART, X_SOL, X_Y, X_FACES, X_FINAL, X_IDX2, X_BASE2, X_COUNT = 0, 1, 2, 3, 4, 5, 6, 9, 12, 15, 16, 17, 18, 19
 
 
 def dot(a, b):
@@ -26,7 +27,7 @@
 
 def kernel(rhs_hbm, bs_hbm, inv_hbm, cc_hbm, idx_hbm, sinv_hbm, out_ref, sep_ref,
            rhs, bs, inv, cc, idx, w, tst, gm, gs, gi, pto, ptb, pta, ptz, stage, kb, pbuf, pout, sbuf, yout, yin,
-           bst, fstage, fk, acca, accb, stot, lsem, ssem, rsem, rs, rr):
+           bst, hstage, hk, fstage, fk, acca, accb, stot, lsem, ssem, rsem, rs, rr):
     p = lax.axis_index("panel")
     front = lax.axis_index("front")
     x, z, c = front // 16, lax.rem(front // 2, 8), lax.rem(front, 2)
@@ -40,8 +41,7 @@
         return other, (p, (x * 8 + other) * 2 + c)
 
     def g_peer(k, panel):
-        other = lax.rem(g + k, 8)
-        return panel, ((other // 2) * 8 + z) * 2 + lax.rem(other, 2)
+        return panel, (lax.rem(x + k // 2, 4) * 8 + z) * 2 + lax.rem(c + k % 2, 2)
 
     def load(src, dst, number):
         copy = pltpu.make_async_copy(src, dst, lsem.at[number])
@@ -79,7 +79,6 @@
             greet(g_peer(k, p + 1))
 
     bst[...] = jnp.zeros((2, FACE, 32), F32)
-    pl.semaphore_wait(barrier, 14 + jnp.where(p > 0, 8, 0) + jnp.where(p < 3, 8, 0))
 
     def send(src, dst, which, device):
         pltpu.make_async_remote_copy(
@@ -88,6 +87,8 @@
 
     def wait(ref, sem):
         pltpu.make_async_copy(ref, ref, sem).wait()
+
+    onto = jnp.where(c == 0, 1, 7)
 
     def block_of(slot, owner):
         return gs.at[:, owner] if slot == R_SINV else gm.at[slot, owner]
@@ -97,10 +98,10 @@
             if step < steps:
                 if step > 0:
                     wait(block_of(slot, 0), rr.at[slot, way, step - 1])
-                owner = lax.rem(z + (8 - step if way == 0 else step), 8)
+                owner = lax.rem(z + step * (8 - onto if way == 0 else onto), 8)
                 pltpu.make_async_remote_copy(
                     src_ref=block_of(slot, owner), dst_ref=block_of(slot, owner), send_sem=rs.at[slot, way, step],
-                    recv_sem=rr.at[slot, way, step], device_id=z_peer(1 if way == 0 else 7)[1], device_id_type=MESH
+                    recv_sem=rr.at[slot, way, step], device_id=z_peer(onto if way == 0 else 8 - onto)[1], device_id_type=MESH
                 ).start()
 
     def ring_end(slot):
@@ -113,8 +114,8 @@
                 wait(block_of(slot, 0), rs.at[slot, way, step])
 
     def first_set(step):
+        ring(S_T, step)
         ring(S_O, step)
-        ring(S_T, step)
 
         @pl.when(p > 0)
         def _():
@@ -124,27 +125,31 @@
         for slot in SECOND_SET:
             ring(slot, step)
 
-    load_sinv.wait()
-    ring(R_SINV, 0)
-    load_idx.wait()
-    own_index = jnp.broadcast_to(idx[...], (8, FACE))
-    gi[z, 0] = own_index
-
-    @pl.when(p == 0)
-    def _():
-        gi[z, 2] = own_index
-
-    @pl.when(p == 3)
-    def _():
-        gi[z, 1] = own_index
-
-    @pl.when(p < 3)
-    def _():
-        send(gi.at[z, 0], gi.at[z, 2], X_UP, (p + 1, front))
-
-    @pl.when(p > 0)
-    def _():
-        send(gi.at[z, 0], gi.at[z, 1], X_DOWN, (p - 1, front))
+    def begin():
+        pl.semaphore_wait(barrier, 14 + jnp.where(p > 0, 8, 0) + jnp.where(p < 3, 8, 0))
+        load_sinv.wait()
+        ring(R_SINV, 0)
+        load_idx.wait()
+        own_index = idx[...]
+        gi[z, 0] = own_index
+        for k in Z_ORDER:
+            send(gi.at[z, 0], gi.at[z, 0], X_IDX, z_peer(k)[1])
+
+        @pl.when(p == 0)
+        def _():
+            gi[z, 2] = own_index
+
+        @pl.when(p == 3)
+        def _():
+            gi[z, 1] = own_index
+
+        @pl.when(p < 3)
+        def _():
+            send(gi.at[z, 0], gi.at[z, 2], X_UP, (p + 1, front))
+
+        @pl.when(p > 0)
+        def _():
+            send(gi.at[z, 0], gi.at[z, 1], X_DOWN, (p - 1, front))
 
     load_cc.wait()
     load_rhs.wait()
@@ -170,13 +175,15 @@
             faces[side] = faces[side] + dot(some, both)
         if block == 0:
             tst[0] = part[:FACE]
+        if block == 1:
+            begin()
 
             @pl.when(p > 0)
             def _():
                 send(tst.at[0], gm.at[S_T, z], X_T, (p - 1, front))
-        if block == 1:
+        if block == 3:
             ring(R_SINV, 1)
-
+        if block == 4:
             @pl.when(p > 0)
             def _():
                 wait(gi.at[0, 0], rsem.at[X_UP])
@@ -185,10 +192,8 @@
             def _():
                 wait(gi.at[0, 0], rsem.at[X_DOWN])
 
-            for k in range(1, 8):
-                send(gi.at[z], gi.at[z], X_IDX, z_peer(k)[1])
-        if block == 3:
-            ring(R_SINV, 2)
+            for k in Z_ORDER:
+                send(gi.at[z, pl.ds(1, 2)], gi.at[z, pl.ds(1, 2)], X_IDX2, z_peer(k)[1])
     tst[1] = w[pl.ds(CELLS - FACE, FACE)]
 
     def combine(value):
@@ -202,26 +207,41 @@
         bst[part, place] = bs[part]
     given = jnp.concatenate([jnp.transpose(bst[0]), jnp.transpose(bst[1])], axis=0)
     face_first, face_last = combine(faces[0]), combine(faces[1])
-    pieces = [combine(towards), given, jnp.where(p < 3, face_last, face_first), face_first]
-    for other in range(8):
-        for item, value in enumerate(pieces):
+
+    def put(item, value):
+        for other in range(8):
             stage[other, item] = jnp.concatenate(
                 [value[4 * other : 4 * other + 4], value[32 + 4 * other : 36 + 4 * other]], axis=0
             )
-    for k in range(1, 8):
+
+    put(0, combine(towards))
+    put(1, given)
+    for k in Z_ORDER:
         other, device = z_peer(k)
-        send(stage.at[other], kb.at[z], X_BASE, device)
+        send(stage.at[other, pl.ds(0, 2)], kb.at[z, pl.ds(0, 2)], X_BASE, device)
+
+    @pl.when(p == 2)
+    def _():
+        send(tst.at[1], gm.at[S_T, z], X_T, (3, front))
+
+    @pl.when(p < 2)
+    def _():
+        send(tst.at[1], gm.at[S_T2, z], X_T2, (p + 1, front))
+
+    ring(R_SINV, 2)
+    wait(gm.at[S_T, 0], rsem.at[X_T])
+
+    @pl.when(p > 0)
+    def _():
+        ring(S_T, 0)
+
+    ahead_t = gm[S_T, z]
+    put(2, jnp.where(p < 3, face_last, face_first))
+    put(3, jnp.where(p == 0, combine(dot(face_last.astype(BF16), ahead_t)), face_first))
+    for k in Z_ORDER:
+        other, device = z_peer(k)
+        send(stage.at[other, pl.ds(2, 2)], kb.at[z, pl.ds(2, 2)], X_BASE2, device)
     kb[z] = stage[z]
-
-    @pl.when(p == 2)
-    def _():
-        send(tst.at[1], gm.at[S_T, z], X_T, (3, front))
-
-    @pl.when(p < 2)
-    def _():
-        send(tst.at[1], gm.at[S_T2, z], X_T2, (p + 1, front))
-
-    ring(R_SINV, 3)
     outs = []
     for side, start in enumerate(starts):
         total = jnp.zeros((2 * FACE, 2 * FACE), F32)
@@ -243,19 +263,33 @@
     gm[S_DFF, z] = d_ff
     gm[S_D2, z] = jnp.concatenate([inv[0, high, low], inv[1, high, low]], axis=1)
     gm[S_D, z] = jnp.where(p < 3, jnp.concatenate([inv[0, low, high], inv[1, low, high]], axis=1), d_ff)
-    wait(gm.at[S_T, 0], rsem.at[X_T])
-    first_set(0)
+    ring(R_SINV, 3)
+
+    @pl.when(p == 0)
+    def _():
+        tall = jnp.concatenate([outs[1][:, :FACE], outs[1][:, FACE:]], axis=0).astype(BF16)
+        both = dot(tall, ahead_t)
+        gm[S_T, z] = jnp.concatenate(
+            [both[:FACE, :FACE] - both[FACE:, FACE:], both[FACE:, :FACE] + both[:FACE, FACE:]], axis=1
+        ).astype(BF16)
+        ring(S_T, 0)
+
+    ring(S_O, 0)
+
+    @pl.when(p > 0)
+    def _():
+        ring(S_D, 0)
 
     unknown = lax.broadcasted_iota(jnp.int32, (SEP, FACE), 0)
 
     def select(dst, item, by_row=False):
         for leaf in range(8):
-            row = gi[leaf, item][0:1, :]
+            row = gi[leaf, item]
             if by_row:
                 row = ((row >> 8) * 2 + ((row >> 4) & 1)) * 128 + ((row >> 5) & 7) * 16 + (row & 15)
             dst[:, leaf * FACE : (leaf + 1) * FACE] = jnp.where(unknown == row, 1.0, 0.0).astype(BF16)
 
-    wait(gi.at[pl.ds(0, 7)], rsem.at[X_IDX])
+    wait(gi.at[pl.ds(0, 7), 0], rsem.at[X_IDX])
     select(ptb, 0)
 
     sign = jnp.where(lax.broadcasted_iota(jnp.int32, (8, SEP), 0) < 4, -1.0, 1.0)
@@ -290,7 +324,7 @@
         both = lax.dot_general(reduced, gs[...].reshape(2 * FACE, SEP), NT, preferred_element_type=F32)
         mine = both[:, :FACE] + sign[:, :FACE] * jnp.roll(both[:, FACE:], 4, axis=0)
         sbuf[turn, g] = mine
-        for k in range(1, 8):
+        for k in G_ORDER[:7]:
             send(sbuf.at[turn, g], sbuf.at[turn, g], X_SOL + turn, g_peer(k, p))
         meanwhile()
         wait(sbuf.at[turn, pl.ds(0, 7)], rsem.at[X_SOL + turn])
@@ -299,12 +333,23 @@
     def onward(face, matrix, slot, which, turn, panel):
         face_low = face.astype(BF16)
         pout[which] = fold(-scatter(leafwise(face_low, slot), matrix))
-        for k in range(8):
+        for k in G_ORDER:
             send(pout.at[which], pbuf.at[turn, g], X_PART + turn, g_peer(k, panel))
         yout[which] = fold(face)
         send(yout.at[which], yin.at[turn], X_Y + turn, (panel, front))
 
-    wait(kb.at[pl.ds(0, 7)], rsem.at[X_BASE])
+    def faces_back():
+        for item in range(2):
+            face = unfold(yin[item + 1])
+            for leaf in range(8):
+                hstage[leaf, item] = face[:, leaf * FACE : (leaf + 1) * FACE]
+        for k in Z_ORDER:
+            other, device = z_peer(k)
+            send(hstage.at[other], hk.at[z], X_FACES, device)
+        hk[z] = hstage[z]
+
+    first_set(1)
+    wait(kb.at[pl.ds(0, 7), pl.ds(0, 2)], rsem.at[X_BASE])
     own = -scatter(jnp.concatenate([kb[leaf, 0] for leaf in range(8)], axis=1), ptb)
     given_low = (kb[0, 1] + kb[1, 1]) + (kb[2, 1] + kb[3, 1])
     given_high = (kb[4, 1] + kb[5, 1]) + (kb[6, 1] + kb[7, 1])
@@ -312,10 +357,8 @@
         [jnp.where(x == other // 2, given_low if other % 2 == 0 else given_high, 0.0) for other in range(8)], axis=1
     )
     pbuf[0, g] = fold(own)
-    for k in range(1, 8):
+    for k in G_ORDER[:7]:
         send(pbuf.at[0, g], pbuf.at[0, g], X_PART, g_peer(k, p))
-    acca[...] = jnp.concatenate([kb[leaf, 2] for leaf in range(8)], axis=1)
-    accb[...] = jnp.concatenate([kb[leaf, 3] for leaf in range(8)], axis=1)
 
     @pl.when(p == 0)
     def _():
@@ -327,10 +370,12 @@
 
     def base_before():
         select(pto, 0, by_row=True)
-        first_set(1)
         ring_end(R_SINV)
+        first_set(2)
 
     def base_meanwhile():
+        wait(gi.at[pl.ds(0, 7), pl.ds(1, 2)], rsem.at[X_IDX2])
+
         @pl.when(p < 3)
         def _():
             select(pta, 1)
@@ -339,10 +384,12 @@
         def _():
             select(pta, 2)
 
-        first_set(2)
+        first_set(3)
+        wait(kb.at[pl.ds(0, 7), pl.ds(2, 2)], rsem.at[X_BASE2])
+        acca[...] = jnp.concatenate([kb[leaf, 2] for leaf in range(8)], axis=1)
+        accb[...] = jnp.concatenate([kb[leaf, 3] for leaf in range(8)], axis=1)
 
     stot[...] = solve(0, 7, base_before, base_meanwhile)
-    first_set(3)
 
     @pl.when(middle)
     def _():
@@ -359,9 +406,22 @@
 
         stot[...] += solve(1, 8, lambda: None, meanwhile)
 
-    ring_end(S_O)
-    ring_end(S_T)
-    onward(acca[...] - leafwise(gather(stot[...]).astype(BF16), S_O), pta, S_T, 0, turn_ahead, ahead)
+    @pl.when(p == 0)
+    def _():
+        pick = gather(stot[...]).astype(BF16)
+        ring_end(S_T)
+        pout[0] = fold(scatter(leafwise(pick, S_T) - accb[...], pta))
+        for k in G_ORDER:
+            send(pout.at[0], pbuf.at[1, g], X_PART + 1, g_peer(k, 1))
+        ring_end(S_O)
+        yout[0] = fold(acca[...] - leafwise(pick, S_O))
+        send(yout.at[0], yin.at[1], X_Y + 1, (1, front))
+
+    @pl.when(p > 0)
+    def _():
+        ring_end(S_O)
+        ring_end(S_T)
+        onward(acca[...] - leafwise(gather(stot[...]).astype(BF16), S_O), pta, S_T, 0, turn_ahead, ahead)
 
     @pl.when(middle)
     def _():
@@ -376,6 +436,7 @@
     def _():
         def meanwhile():
             wait(yin.at[2], rsem.at[X_Y + 2])
+            faces_back()
 
             @pl.when(p > 0)
             def _():
@@ -383,43 +444,42 @@
 
         stot[...] += solve(2, 8, lambda: None, meanwhile)
 
+    @pl.when(p == 3)
+    def _():
+        faces_back()
+
     picked = gather(stot[...])
 
     @pl.when(middle)
     def _():
         onward(accb[...] - leafwise(picked.astype(BF16), S_O2), ptz, S_T2, 1, 2, p - 1)
 
-    low_face, high_face = unfold(yin[1]), unfold(yin[2])
     own_sep = sbuf[0, g]
     own_sep = own_sep + jnp.where(p > 0, sbuf[1, g], 0.0)
     own_sep = own_sep + jnp.where(p < 3, sbuf[2, g], 0.0)
     for leaf in range(8):
         cols = slice(leaf * FACE, (leaf + 1) * FACE)
         fstage[leaf, 0] = picked[:, cols]
-        fstage[leaf, 1] = low_face[:, cols]
-        fstage[leaf, 2] = high_face[:, cols]
-        fstage[leaf, 3] = own_sep
-    for k in range(1, 8):
+        fstage[leaf, 1] = own_sep
+    for k in Z_ORDER:
         other, device = z_peer(k)
         send(fstage.at[other], fk.at[z], X_FINAL, device)
     fk[z] = fstage[z]
+
+    def rows_of(ref, item):
+        tops = [ref[other, item][:4] for other in range(8)]
+        bottoms = [ref[other, item][4:] for other in range(8)]
+        return jnp.concatenate(tops, axis=0), jnp.concatenate(bottoms, axis=0)
+
+    wait(hk.at[pl.ds(0, 7)], rsem.at[X_FACES])
+    add_low = jnp.concatenate(rows_of(hk, 0), axis=0)
+    add_high = jnp.concatenate(rows_of(hk, 1), axis=0)
     wait(fk.at[pl.ds(0, 7)], rsem.at[X_FINAL])
-
-    def rows_of(item):
-        tops = [fk[other, item][:4] for other in range(8)]
-        bottoms = [fk[other, item][4:] for other in range(8)]
-        return jnp.concatenate(tops, axis=0), jnp.concatenate(bottoms, axis=0)
-
-    for part, value in enumerate(rows_of(3)):
-        bst[part] = jnp.transpose(value)
-        sep_ref[part] = bst[part, pl.ds(pl.multiple_of(z * 16, 16), 16)]
-    pick_re, pick_im = rows_of(0)
+    pick_re, pick_im = rows_of(fk, 0)
     doubled = jnp.concatenate(
         [jnp.concatenate([pick_re, -pick_im], axis=1), jnp.concatenate([pick_im, pick_re], axis=1)], axis=0
     ).astype(BF16)
     side = rhs[...].reshape(64, CELLS) - lax.dot_general(doubled, link, NT, preferred_element_type=F32)
-    add_low = jnp.concatenate(rows_of(1), axis=0)
-    add_high = jnp.concatenate(rows_of(2), axis=0)
     side = jnp.concatenate(
         [side[:, :FACE] + add_low, side[:, FACE : CELLS - FACE], side[:, CELLS - FACE :] + add_high], axis=1
     ).astype(BF16)
@@ -430,11 +490,18 @@
         out_ref[0, :, cols] = real[:32] - imag[32:]
         out_ref[1, :, cols] = real[32:] + imag[:32]
 
+    for part, value in enumerate(rows_of(fk, 1)):
+        bst[part] = jnp.transpose(value)
+        sep_ref[part] = bst[part, pl.ds(pl.multiple_of(z * 16, 16), 16)]
+
     ring_left(R_SINV)
     ring_left(S_O)
     ring_left(S_T)
-    wait(gi.at[pl.ds(0, 7)], ssem.at[X_IDX])
-    wait(kb.at[pl.ds(0, 7)], ssem.at[X_BASE])
+    wait(gi.at[pl.ds(0, 7), 0], ssem.at[X_IDX])
+    wait(gi.at[pl.ds(0, 7), pl.ds(1, 2)], ssem.at[X_IDX2])
+    wait(kb.at[pl.ds(0, 7), pl.ds(0, 2)], ssem.at[X_BASE])
+    wait(kb.at[pl.ds(0, 7), pl.ds(0, 2)], ssem.at[X_BASE2])
+    wait(hk.at[pl.ds(0, 7)], ssem.at[X_FACES])
     wait(fk.at[pl.ds(0, 7)], ssem.at[X_FINAL])
     wait(pbuf.at[0, pl.ds(0, 7)], ssem.at[X_PART])
     wait(sbuf.at[0, pl.ds(0, 7)], ssem.at[X_SOL])
@@ -490,7 +557,7 @@
             pltpu.VMEM((2, FACE, 2 * FACE), BF16),
             pltpu.VMEM((7, 8, FACE, 2 * FACE), BF16),
             pltpu.VMEM((2, 8, 16, SEP), BF16),
-            pltpu.VMEM((8, 3, 8, FACE), jnp.int32),
+            pltpu.VMEM((8, 3, 1, FACE), jnp.int32),
             pltpu.VMEM((SEP, SEP), BF16),
             pltpu.VMEM((SEP, SEP), BF16),
             pltpu.VMEM((SEP, SEP), BF16),
@@ -503,8 +570,10 @@
             pltpu.VMEM((2, 16, SEP // 2), BF16),
             pltpu.VMEM((3, 16, SEP // 2), BF16),
             pltpu.VMEM((2, FACE, 32), F32),
-            pltpu.VMEM((8, 4, 8, FACE), F32),
-            pltpu.VMEM((8, 4, 8, FACE), F32),
+            pltpu.VMEM((8, 2, 8, FACE), F32),
+            pltpu.VMEM((8, 2, 8, FACE), F32),
+            pltpu.VMEM((8, 2, 8, FACE), F32),
+            pltpu.VMEM((8, 2, 8, FACE), F32),
             pltpu.VMEM((8, SEP), F32),
             pltpu.VMEM((8, SEP), F32),
             pltpu.VMEM((8, SEP), F32),

time: 113 us -> 110 us (0.973)
  Pallas kernels: 110 us -> 106 us
    pallas_call x1, Pallas kernels: 110 us -> 106 us  [local(): pl.pallas_call(kernel, out_shape=(jax.ShapeDtypeStruct((2, 32, CELLS), F3...]
where the time goes in v3:
time: 110 us
  Pallas kernels  106 us (96%)
  local copies, waits for them, and re-layouts  3.04 us (3%)
    pallas_call x1, Pallas kernels, local(): pl.pallas_call(kernel, out_shape=(jax.ShapeDtypeStruct((2, 32, CELLS), F3...  106 us
    unnamed x2, local copies, waits for them, and re-layouts  3.04 us

profile of v3, /device:TPU:1, one launch (start us, length us, event | category | flops | bytes accessed | tf_op | source)
XLA Modules:
  0.0 110.0 jit_solution(1899875285198533910)
XLA Ops:
  0.6 106.3 %shard_map.77 = (f32[2,32,1280]{2,1,0:T(8,128)}, f32[2,16,32]{2,1,0:T(8,128)}) custom-call(f32[2,32,1280]{2,1,0:T(8,128)} %bitcast.16, f32[2,16,32]{2,1,0:T(8,128)} %bitcast.19, bf16[2,1280,1280]{2,1,0:T(8,128)(2,1)} %bitcast.14, bf16[2,1280,128]{2,1,0:T(8,128)(2,1)} %bitcast.15, s32[1,128]{1,0:T(1,128)} %bitcast.21, bf16[2,16,1024]{2,1,0:T(8,128)(2,1)} %bitcast.18), custom_call_target="tpu_custom_call" | custom-call | tf_op jit(solution)/shard_map/pallas_call | solution.py:545
  106.9 1.7 %copy.10 = f32[1,1,2,32,1280]{4,3,2,1,0:T(8,128)} copy(f32[1,1,2,32,1280]{4,3,2,1,0:T(8,128)} %bitcast.17) | data formatting | bytes 655360
  108.6 1.3 %copy.11 = f32[1,2,32,16]{2,3,1,0:T(8,128)} copy(f32[1,2,32,16]{2,3,1,0:T(8,128)} %bitcast.20) | data formatting | bytes 8192

commit v4 on v3

--- a/solution.py
+++ b/solution.py
@@ -27,7 +27,7 @@
 
 def kernel(rhs_hbm, bs_hbm, inv_hbm, cc_hbm, idx_hbm, sinv_hbm, out_ref, sep_ref,
            rhs, bs, inv, cc, idx, w, tst, gm, gs, gi, pto, ptb, pta, ptz, stage, kb, pbuf, pout, sbuf, yout, yin,
-           bst, hstage, hk, fstage, fk, acca, accb, stot, lsem, ssem, rsem, rs, rr):
+           bst, hstage, hk, fstage, fk, acca, accb, acct, stot, got, whole, lsem, ssem, rsem, rs, rr):
     p = lax.axis_index("panel")
     front = lax.axis_index("front")
     x, z, c = front // 16, lax.rem(front // 2, 8), lax.rem(front, 2)
@@ -115,11 +115,12 @@
 
     def first_set(step):
         ring(S_T, step)
+
+        @pl.when(p > 0)
+        def _():
+            ring(S_D, step)
+
         ring(S_O, step)
-
-        @pl.when(p > 0)
-        def _():
-            ring(S_D, step)
 
     def second_set(step):
         for slot in SECOND_SET:
@@ -274,11 +275,11 @@
         ).astype(BF16)
         ring(S_T, 0)
 
+    @pl.when(p > 0)
+    def _():
+        ring(S_D, 0)
+
     ring(S_O, 0)
-
-    @pl.when(p > 0)
-    def _():
-        ring(S_D, 0)
 
     unknown = lax.broadcasted_iota(jnp.int32, (SEP, FACE), 0)
 
@@ -295,7 +296,7 @@
     sign = jnp.where(lax.broadcasted_iota(jnp.int32, (8, SEP), 0) < 4, -1.0, 1.0)
 
     def leafwise(vector, slot):
-        parts = [dot(vector[:, leaf * FACE : (leaf + 1) * FACE], gm[slot, leaf]) for leaf in range(8)]
+        parts = [dot(vector[:, leaf * FACE : (leaf + 1) * FACE], got[leaf] if slot is None else gm[slot, leaf]) for leaf in range(8)]
         direct = jnp.concatenate([v[:, :FACE] for v in parts], axis=1)
         crossed = jnp.concatenate([v[:, FACE:] for v in parts], axis=1)
         return direct + sign * jnp.roll(crossed, 4, axis=0)
@@ -348,6 +349,21 @@
             send(hstage.at[other], hk.at[z], X_FACES, device)
         hk[z] = hstage[z]
 
+    def through(o_slot, t_slot):
+        for leaf in range(8):
+            out = gm[o_slot, leaf]
+            both = dot(jnp.concatenate([out[:, :FACE], out[:, FACE:]], axis=0), gm[t_slot, leaf])
+            got[leaf] = jnp.concatenate(
+                [both[:FACE, :FACE] - both[FACE:, FACE:], both[FACE:, :FACE] + both[:FACE, FACE:]], axis=1
+            ).astype(BF16)
+
+    def onward_folded(pick, acc, matrix, o_slot, which, turn, panel):
+        pout[which] = fold(scatter(leafwise(pick, None) - acct[...], matrix))
+        for k in G_ORDER:
+            send(pout.at[which], pbuf.at[turn, g], X_PART + turn, g_peer(k, panel))
+        yout[which] = fold(acc[...] - leafwise(pick, o_slot))
+        send(yout.at[which], yin.at[turn], X_Y + turn, (panel, front))
+
     first_set(1)
     wait(kb.at[pl.ds(0, 7), pl.ds(0, 2)], rsem.at[X_BASE])
     own = -scatter(jnp.concatenate([kb[leaf, 0] for leaf in range(8)], axis=1), ptb)
@@ -391,7 +407,7 @@
 
     stot[...] = solve(0, 7, base_before, base_meanwhile)
 
-    @pl.when(middle)
+    @pl.when(p == 2)
     def _():
         wait(gm.at[S_T2, 0], rsem.at[X_T2])
         second_set(0)
@@ -403,6 +419,16 @@
             wait(yin.at[1], rsem.at[X_Y + 1])
             ring_end(S_D)
             acca[...] += leafwise(unfold(yin[1]).astype(BF16), S_D)
+
+            @pl.when(p > 1)
+            def _():
+                acct[...] = leafwise(acca[...].astype(BF16), S_T)
+
+        @pl.when(p > 1)
+        def _():
+            ring_end(S_O)
+            ring_end(S_T)
+            through(S_O, S_T)
 
         stot[...] += solve(1, 8, lambda: None, meanwhile)
 
@@ -416,12 +442,34 @@
         ring_end(S_O)
         yout[0] = fold(acca[...] - leafwise(pick, S_O))
         send(yout.at[0], yin.at[1], X_Y + 1, (1, front))
-
-    @pl.when(p > 0)
+        sides = rhs[...].reshape(64, CELLS).astype(BF16)
+        links = jnp.concatenate([cc[0], cc[1]], axis=1)
+        for block in range(5):
+            cols = pl.ds(block * BLOCK, BLOCK)
+            real = dot(sides, inv[0, :, cols])
+            imag = dot(sides, inv[1, :, cols])
+            out_ref[0, :, cols] = real[:32] - imag[32:]
+            out_ref[1, :, cols] = real[32:] + imag[:32]
+            by_real = lax.dot_general(links, inv[0, :, cols], TN, preferred_element_type=F32)
+            by_imag = lax.dot_general(links, inv[1, :, cols], TN, preferred_element_type=F32)
+            whole[:FACE, cols] = (by_real[:FACE] - by_imag[FACE:]).astype(BF16)
+            whole[FACE:, cols] = (by_imag[:FACE] + by_real[FACE:]).astype(BF16)
+
+    @pl.when(p == 1)
     def _():
         ring_end(S_O)
         ring_end(S_T)
-        onward(acca[...] - leafwise(gather(stot[...]).astype(BF16), S_O), pta, S_T, 0, turn_ahead, ahead)
+        onward(acca[...] - leafwise(gather(stot[...]).astype(BF16), S_O), pta, S_T, 0, 1, 2)
+
+    @pl.when(p > 1)
+    def _():
+        onward_folded(gather(stot[...]).astype(BF16), acca, pta, S_O, 0, turn_ahead, ahead)
+
+    @pl.when(p == 1)
+    def _():
+        wait(gm.at[S_T2, 0], rsem.at[X_T2])
+        second_set(0)
+        second_set(1)
 
     @pl.when(middle)
     def _():
@@ -431,6 +479,7 @@
         for slot in SECOND_SET:
             ring_end(slot)
         accb[...] += leafwise(unfold(yin[1]).astype(BF16), S_DFF)
+        through(S_O2, S_T2)
 
     @pl.when(p < 3)
     def _():
@@ -441,6 +490,7 @@
             @pl.when(p > 0)
             def _():
                 accb[...] += leafwise(unfold(yin[2]).astype(BF16), S_D2)
+                acct[...] = leafwise(accb[...].astype(BF16), S_T2)
 
         stot[...] += solve(2, 8, lambda: None, meanwhile)
 
@@ -452,7 +502,7 @@
 
     @pl.when(middle)
     def _():
-        onward(accb[...] - leafwise(picked.astype(BF16), S_O2), ptz, S_T2, 1, 2, p - 1)
+        onward_folded(picked.astype(BF16), accb, ptz, S_O2, 1, 2, p - 1)
 
     own_sep = sbuf[0, g]
     own_sep = own_sep + jnp.where(p > 0, sbuf[1, g], 0.0)
@@ -471,24 +521,48 @@
         bottoms = [ref[other, item][4:] for other in range(8)]
         return jnp.concatenate(tops, axis=0), jnp.concatenate(bottoms, axis=0)
 
+    def doubled(ref, item):
+        re, im = rows_of(ref, item)
+        return jnp.concatenate(
+            [jnp.concatenate([re, -im], axis=1), jnp.concatenate([im, re], axis=1)], axis=0
+        ).astype(BF16)
+
     wait(hk.at[pl.ds(0, 7)], rsem.at[X_FACES])
-    add_low = jnp.concatenate(rows_of(hk, 0), axis=0)
-    add_high = jnp.concatenate(rows_of(hk, 1), axis=0)
+
+    @pl.when(p == 0)
+    def _():
+        face = doubled(hk, 1)
+        for block in range(5):
+            cols = pl.ds(block * BLOCK, BLOCK)
+            both = dot(face, jnp.concatenate([inv[0, high, cols], inv[1, high, cols]], axis=0))
+            out_ref[0, :, cols] += both[:32]
+            out_ref[1, :, cols] += both[32:]
+
     wait(fk.at[pl.ds(0, 7)], rsem.at[X_FINAL])
-    pick_re, pick_im = rows_of(fk, 0)
-    doubled = jnp.concatenate(
-        [jnp.concatenate([pick_re, -pick_im], axis=1), jnp.concatenate([pick_im, pick_re], axis=1)], axis=0
-    ).astype(BF16)
-    side = rhs[...].reshape(64, CELLS) - lax.dot_general(doubled, link, NT, preferred_element_type=F32)
-    side = jnp.concatenate(
-        [side[:, :FACE] + add_low, side[:, FACE : CELLS - FACE], side[:, CELLS - FACE :] + add_high], axis=1
-    ).astype(BF16)
-    for block in range(5):
-        cols = pl.ds(block * BLOCK, BLOCK)
-        real = dot(side, inv[0, :, cols])
-        imag = dot(side, inv[1, :, cols])
-        out_ref[0, :, cols] = real[:32] - imag[32:]
-        out_ref[1, :, cols] = real[32:] + imag[:32]
+
+    @pl.when(p == 0)
+    def _():
+        both = dot(doubled(fk, 0), whole[...])
+        out_ref[0] -= both[:32]
+        out_ref[1] -= both[32:]
+
+    @pl.when(p > 0)
+    def _():
+        links = jnp.concatenate([cc[0], cc[1]], axis=1)
+        side = rhs[...].reshape(64, CELLS) - lax.dot_general(
+            doubled(fk, 0), links, NT, preferred_element_type=F32
+        )
+        add_low = jnp.concatenate(rows_of(hk, 0), axis=0)
+        add_high = jnp.concatenate(rows_of(hk, 1), axis=0)
+        side = jnp.concatenate(
+            [side[:, :FACE] + add_low, side[:, FACE : CELLS - FACE], side[:, CELLS - FACE :] + add_high], axis=1
+        ).astype(BF16)
+        for block in range(5):
+            cols = pl.ds(block * BLOCK, BLOCK)
+            real = dot(side, inv[0, :, cols])
+            imag = dot(side, inv[1, :, cols])
+            out_ref[0, :, cols] = real[:32] - imag[32:]
+            out_ref[1, :, cols] = real[32:] + imag[:32]
 
     for part, value in enumerate(rows_of(fk, 1)):
         bst[part] = jnp.transpose(value)
@@ -577,6 +651,9 @@
             pltpu.VMEM((8, SEP), F32),
             pltpu.VMEM((8, SEP), F32),
             pltpu.VMEM((8, SEP), F32),
+            pltpu.VMEM((8, SEP), F32),
+            pltpu.VMEM((8, FACE, 2 * FACE), BF16),
+            pltpu.VMEM((2 * FACE, CELLS), BF16),
             pltpu.SemaphoreType.DMA((10,)),
             pltpu.SemaphoreType.DMA((X_COUNT,)),
             pltpu.SemaphoreType.DMA((X_COUNT,)),

time: 110 us -> 105 us (0.955)
  Pallas kernels: 106 us -> 101 us
    pallas_call x1, Pallas kernels: 106 us -> 101 us  [local(): pl.pallas_call(kernel, out_shape=(jax.ShapeDtypeStruct((2, 32, CELLS), F3...]
where the time goes in v4:
time: 105 us
  Pallas kernels  101 us (96%)
  local copies, waits for them, and re-layouts  3.04 us (3%)
    pallas_call x1, Pallas kernels, local(): pl.pallas_call(kernel, out_shape=(jax.ShapeDtypeStruct((2, 32, CELLS), F3...  101 us
    unnamed x2, local copies, waits for them, and re-layouts  3.04 us

profile of v4, /device:TPU:1, one launch (start us, length us, event | category | flops | bytes accessed | tf_op | source)
XLA Modules:
  0.0 104.8 jit_solution(8702589526360158768)
XLA Ops:
  0.6 101.1 %shard_map.77 = (f32[2,32,1280]{2,1,0:T(8,128)}, f32[2,16,32]{2,1,0:T(8,128)}) custom-call(f32[2,32,1280]{2,1,0:T(8,128)} %bitcast.16, f32[2,16,32]{2,1,0:T(8,128)} %bitcast.19, bf16[2,1280,1280]{2,1,0:T(8,128)(2,1)} %bitcast.14, bf16[2,1280,128]{2,1,0:T(8,128)(2,1)} %bitcast.15, s32[1,128]{1,0:T(1,128)} %bitcast.21, bf16[2,16,1024]{2,1,0:T(8,128)(2,1)} %bitcast.18), custom_call_target="tpu_custom_call" | custom-call | tf_op jit(solution)/shard_map/pallas_call | solution.py:619
  101.7 1.7 %copy.10 = f32[1,1,2,32,1280]{4,3,2,1,0:T(8,128)} copy(f32[1,1,2,32,1280]{4,3,2,1,0:T(8,128)} %bitcast.17) | data formatting | bytes 655360
  103.4 1.3 %copy.11 = f32[1,2,32,16]{2,3,1,0:T(8,128)} copy(f32[1,2,32,16]{2,3,1,0:T(8,128)} %bitcast.20) | data formatting | bytes 8192

commit v5 on v4

--- a/solution.py
+++ b/solution.py
@@ -15,7 +15,7 @@
 NT = (((1,), (1,)), ((), ()))
 TN = (((0,), (0,)), ((), ()))
 
-S_T, S_O, S_D, S_O2, S_T2, S_D2, S_DFF, R_SINV = range(8)
+S_T, S_O, S_D, S_O2, S_T2, S_D2, S_DFF, R_SINV, R_SINV2 = range(9)
 Z_ORDER, G_ORDER = (4, 3, 5, 2, 6, 1, 7), (4, 5, 2, 6, 3, 7, 1, 0)
 FIRST_SET, SECOND_SET = (S_O, S_T, S_D), (S_O2, S_T2, S_D2, S_DFF)
 X_UP, X_DOWN, X_IDX, X_BASE, X_T, X_T2, X_PART, X_SOL, X_Y, X_FACES, X_FINAL, X_IDX2, X_BASE2, X_COUNT = 0, 1, 2, 3, 4, 5, 6, 9, 12, 15, 16, 17, 18, 19
@@ -91,7 +91,7 @@
     onto = jnp.where(c == 0, 1, 7)
 
     def block_of(slot, owner):
-        return gs.at[:, owner] if slot == R_SINV else gm.at[slot, owner]
+        return gs.at[slot - R_SINV, owner] if slot >= R_SINV else gm.at[slot, owner]
 
     def ring(slot, step):
         for way, steps in ((0, 4), (1, 3)):
@@ -130,6 +130,7 @@
         pl.semaphore_wait(barrier, 14 + jnp.where(p > 0, 8, 0) + jnp.where(p < 3, 8, 0))
         load_sinv.wait()
         ring(R_SINV, 0)
+        ring(R_SINV2, 0)
         load_idx.wait()
         own_index = idx[...]
         gi[z, 0] = own_index
@@ -184,6 +185,7 @@
                 send(tst.at[0], gm.at[S_T, z], X_T, (p - 1, front))
         if block == 3:
             ring(R_SINV, 1)
+            ring(R_SINV2, 1)
         if block == 4:
             @pl.when(p > 0)
             def _():
@@ -230,6 +232,7 @@
         send(tst.at[1], gm.at[S_T2, z], X_T2, (p + 1, front))
 
     ring(R_SINV, 2)
+    ring(R_SINV2, 2)
     wait(gm.at[S_T, 0], rsem.at[X_T])
 
     @pl.when(p > 0)
@@ -265,6 +268,7 @@
     gm[S_D2, z] = jnp.concatenate([inv[0, high, low], inv[1, high, low]], axis=1)
     gm[S_D, z] = jnp.where(p < 3, jnp.concatenate([inv[0, low, high], inv[1, low, high]], axis=1), d_ff)
     ring(R_SINV, 3)
+    ring(R_SINV2, 3)
 
     @pl.when(p == 0)
     def _():
@@ -387,6 +391,7 @@
     def base_before():
         select(pto, 0, by_row=True)
         ring_end(R_SINV)
+        ring_end(R_SINV2)
         first_set(2)
 
     def base_meanwhile():
@@ -569,6 +574,7 @@
         sep_ref[part] = bst[part, pl.ds(pl.multiple_of(z * 16, 16), 16)]
 
     ring_left(R_SINV)
+    ring_left(R_SINV2)
     ring_left(S_O)
     ring_left(S_T)
     wait(gi.at[pl.ds(0, 7), 0], ssem.at[X_IDX])
@@ -657,8 +663,8 @@
             pltpu.SemaphoreType.DMA((10,)),
             pltpu.SemaphoreType.DMA((X_COUNT,)),
             pltpu.SemaphoreType.DMA((X_COUNT,)),
-            pltpu.SemaphoreType.DMA((8, 2, 4)),
-            pltpu.SemaphoreType.DMA((8, 2, 4)),
+            pltpu.SemaphoreType.DMA((9, 2, 4)),
+            pltpu.SemaphoreType.DMA((9, 2, 4)),
         ],
         compiler_params=pltpu.CompilerParams(
             collective_id=0, has_side_effects=True, vmem_limit_bytes=56 * 2**20

time: 105 us -> 104 us (level)
  Pallas kernels: 101 us -> 99.7 us
    pallas_call x1, Pallas kernels: 101 us -> 99.7 us  [local(): pl.pallas_call(kernel, out_shape=(jax.ShapeDtypeStruct((2, 32, CELLS), F3...]
where the time goes in v5:
time: 104 us; the launch traced here: 103 us
  Pallas kernels  99.7 us (96%)
  local copies, waits for them, and re-layouts  3.04 us (3%)
    pallas_call x1, Pallas kernels, local(): pl.pallas_call(kernel, out_shape=(jax.ShapeDtypeStruct((2, 32, CELLS), F3...  99.7 us
    unnamed x2, local copies, waits for them, and re-layouts  3.04 us

profile of v5, /device:TPU:1, one launch (start us, length us, event | category | flops | bytes accessed | tf_op | source)
XLA Modules:
  0.0 103.3 jit_solution(4304602101153983552)
XLA Ops:
  0.6 99.7 %shard_map.77 = (f32[2,32,1280]{2,1,0:T(8,128)}, f32[2,16,32]{2,1,0:T(8,128)}) custom-call(f32[2,32,1280]{2,1,0:T(8,128)} %bitcast.16, f32[2,16,32]{2,1,0:T(8,128)} %bitcast.19, bf16[2,1280,1280]{2,1,0:T(8,128)(2,1)} %bitcast.14, bf16[2,1280,128]{2,1,0:T(8,128)(2,1)} %bitcast.15, s32[1,128]{1,0:T(1,128)} %bitcast.21, bf16[2,16,1024]{2,1,0:T(8,128)(2,1)} %bitcast.18), custom_call_target="tpu_custom_call" | custom-call | tf_op jit(solution)/shard_map/pallas_call | solution.py:625
  100.3 1.7 %copy.10 = f32[1,1,2,32,1280]{4,3,2,1,0:T(8,128)} copy(f32[1,1,2,32,1280]{4,3,2,1,0:T(8,128)} %bitcast.17) | data formatting | bytes 655360
  102.0 1.3 %copy.11 = f32[1,2,32,16]{2,3,1,0:T(8,128)} copy(f32[1,2,32,16]{2,3,1,0:T(8,128)} %bitcast.20) | data formatting | bytes 8192
